TPU v7x, 128 devices: a whole 4x4x4 slice. The times are simulated.
128 devices in a mesh: sub: 32 (over x, z, core), crs: 4 (over y).
Axes of the slice: x: 4, y: 4, z: 4, core: 2. Of those that a mesh axis runs over, the one named last changes fastest.
Arguments:
- face_index: int32 [128, 4, 147], P(('sub', 'crs')), may hold values from 0 to 1214, as said below
- kinv: float32 [128, 1215, 1215], P(('sub', 'crs')), as said below
- schur: float32 [128, 588, 588], P(('sub', 'crs'))
- corner: float32 [128, 1215, 24], P(('sub', 'crs')), may hold values from -0.3125 to 0.3125
- coarse_inverse: float32 [744, 744], P('crs')
- loads: float32 [128, 1215, 512], P(('sub', 'crs')), may hold values from -6 to 6
Outputs:
- multipliers: float32 [128, 4, 147, 512], P(('sub', 'crs'))
- residual: float32 [128, 4, 147, 512], P(('sub', 'crs'))
Inputs may be any that keep to these rules, and one draw needn't show every extreme that they name: `face_index`: the 588 entries of one subdomain are distinct rows of its 1215 interface unknowns. kinv, schur and coarse_inverse are symmetric positive definite.
All inputs are finite; a program needn't handle non-finite values.
Results may differ from a plain program's by a relative error of at most 0.0003.
Values sent between devices are 32-bit elements; how exact they have to be, the bound alone decides.
A program may use at most 128 MiB of HBM per device.

v0:
```python
import jax
import jax.numpy as jnp
from jax import lax
from jax.sharding import PartitionSpec as P

ITERS = 2


def padded(cells, sides, width, closed):
    for axis, dim in sides:
        count = lax.axis_size(axis)
        ends = count if closed else count - 1
        head = lax.slice_in_dim(cells, 0, width, axis=dim)
        tail = lax.slice_in_dim(cells, cells.shape[dim] - width, cells.shape[dim], axis=dim)
        cells = jnp.concatenate(
            [
                lax.ppermute(tail, axis, [(i, (i + 1) % count) for i in range(ends)]),
                cells,
                lax.ppermute(head, axis, [((i + 1) % count, i) for i in range(ends)]),
            ],
            axis=dim,
        )
    return cells


def tdot(left, right):
    return lax.dot_general(left, right, (((0,), (0,)), ((), ())), precision=lax.Precision.HIGHEST)


def hdot(left, right):
    return jnp.dot(left, right, precision=lax.Precision.HIGHEST)


def body(face_index, kinv, schur, corner, coarse_inverse, loads):
    rows_idx = face_index[0].reshape(-1)
    kmat = kinv[0]
    smat = schur[0]
    gmat = corner[0]
    nfaces, facedofs = (face_index.shape[1], face_index.shape[2])
    nrows, cases = (loads.shape[1], loads.shape[2])
    coarse_size = coarse_inverse.shape[1]
    nsub = lax.axis_size("sub")
    ncrs = lax.axis_size("crs")
    apos = lax.axis_index("sub")
    bpos = lax.axis_index("crs")
    signs = jnp.array([-1.0, 1.0, -1.0, 1.0], jnp.float32)[:, None, None]
    first = jnp.where(apos > 0, 1.0, 0.0)
    second = jnp.where(apos < nsub - 1, 1.0, 0.0)
    keep = jnp.stack([first, second, jnp.float32(1.0), jnp.float32(1.0)])[:, None, None]
    local = jnp.arange(24, dtype=jnp.int32)
    which = local // 3
    arow = apos + which // 4
    bcol = (bpos + which // 2 % 2) % ncrs
    dof = 3 * (2 * ((arow - 1) * ncrs + bcol) + which % 2) + local % 3
    valid = (arow >= 1) & (arow <= nsub - 1)
    cols = jnp.arange(coarse_size, dtype=jnp.int32)
    emap = jnp.where(valid[:, None] & (dof[:, None] == cols[None, :]), 1.0, 0.0).astype(jnp.float32)

    def assemble(values):
        partial_value = tdot(gmat, values)
        return lax.psum(tdot(emap, partial_value), ("sub", "crs"))

    def coarse(values):
        total = assemble(values)
        solved = lax.all_gather(hdot(coarse_inverse, total), "crs", axis=0, tiled=True)
        return hdot(gmat, hdot(emap, solved))

    def pick(values):
        return values[rows_idx].reshape(nfaces, facedofs, cases)

    def jump(faces):
        pad_sub = padded(faces[0:2], (("sub", 0),), 1, False)
        pad_crs = padded(faces[2:4], (("crs", 0),), 1, True)
        out = jnp.stack(
            [
                -faces[0] + pad_sub[0],
                faces[1] - pad_sub[3],
                -faces[2] + pad_crs[0],
                faces[3] - pad_crs[3],
            ]
        )
        return out * keep

    def operator(values):
        return jump(pick(hdot(kmat, values) + coarse(values)))

    def precond(resid):
        scaled = (0.5 * signs * keep * resid).reshape(nfaces * facedofs, cases)
        return 0.5 * jump(hdot(smat, scaled).reshape(nfaces, facedofs, cases))

    def inner(left, right):
        return lax.psum(0.5 * jnp.sum(left * right, axis=(0, 1)), ("sub", "crs"))

    residual = operator(loads[0])
    multipliers = jnp.zeros_like(residual)
    zvec = precond(residual)
    direction = zvec
    rz_now = inner(residual, zvec)
    for step in range(ITERS):
        image = operator(
            jnp.zeros((nrows, cases), jnp.float32)
            .at[rows_idx]
            .set((signs * direction).reshape(-1, cases))
        )
        alpha = rz_now / inner(direction, image)
        multipliers = multipliers + alpha * direction
        residual = residual - alpha * image
        zvec = precond(residual)
        rz_next = inner(residual, zvec)
        direction = zvec + rz_next / rz_now * direction
        rz_now = rz_next
    return (multipliers[None], residual[None])


def solution(mesh):
    in_specs = (
        P(("sub", "crs"), None, None),
        P(("sub", "crs"), None, None),
        P(("sub", "crs"), None, None),
        P(("sub", "crs"), None, None),
        P("crs", None),
        P(("sub", "crs"), None, None),
    )
    out_specs = (P(("sub", "crs"), None, None, None), P(("sub", "crs"), None, None, None))
    return jax.shard_map(body, mesh=mesh, in_specs=in_specs, out_specs=out_specs, check_vma=False)
```

profile of v0, /device:TPU:1, one launch (start us, length us, event | category | flops | bytes accessed | tf_op | source)
XLA Modules:
  0.0 935.7 jit_solution(971773362120280379)
XLA Ops:
  7.3 3.1 fusion.14
  10.4 2.6 fusion.69
  13.1 152.1 %all-reduce.5.cloned.1.call-done = f32[744,512]{1,0:T(8,128)} async-done(((f32[744,512]{1,0:T(8,128)}), f32[744,512]{1,0:T(8,128)}) %all-reduce.5.cloned.1.call-update) | async-done | bytes 1523728 | tf_op jit(solution)/shard_map/psum | solution.py:61
  165.2 3.4 convolution_bitcast_fusion.3
  168.8 24.8 %all-gather.7.cloned.1.call-done = f32[4,186,512]{2,1,0:T(8,128)} async-done(((f32[1,186,512]{2,1,0:T(8,128)}), f32[4,186,512]{2,1,0:T(8,128)}) %all-gather.7.cloned.1.call-update) | async-done | bytes 1523728 | tf_op jit(solution)/shard_map/all_gather | solution.py:65
  196.1 2.1 convolution_bitcast_fusion
  198.2 12.4 %fusion.9 = f32[1215,512]{1,0:T(8,128)S(1)} fusion(f32[1215,512]{1,0:T(8,128)S(1)} %convolution_bitcast_fusion, f32[1,1215,1215]{2,0,1:T(1,128)} %param.8, f32[1,1215,512]{2,0,1:T(1,128)S(1)} %copy-done.13), kind=kOutput, calls=%fused_computation.16 | convolution fusion | flops 9070548992 | bytes 13369860 | tf_op jit(solution)/shard_map/dot_general | solution.py:31
  210.7 3.0 gather_fusion
  213.7 2.3 slice_bitcast_fusion.9
  216.0 3.7 collective-permute-start
  223.9 4.7 collective-permute-done.1
  235.0 2.5 mul.356
  237.5 4.8 fusion.25
  243.3 5.3 collective-permute-start.4
  252.7 4.3 collective-permute-done.5
  261.6 2.5 stack.108
  264.1 7.3 scatter_custom_fusion
  273.0 2.6 fusion.65
  276.1 149.9 %all-reduce.7.cloned.1.call-done = f32[744,512]{1,0:T(8,128)} async-done(((f32[744,512]{1,0:T(8,128)}), f32[744,512]{1,0:T(8,128)}) %all-reduce.7.cloned.1.call-update) | async-done | bytes 1523728 | tf_op jit(solution)/shard_map/psum | solution.py:61
  426.1 3.4 convolution_bitcast_fusion.2
  429.5 13.5 %fusion.2 = f32[512,1215]{0,1:T(8,128)} fusion(f32[1215,512]{1,0:T(8,128)S(1)} %scatter_custom_fusion, f32[1,1215,1215]{2,0,1:T(1,128)} %param.8), kind=kOutput, calls=%fused_computation.7 | convolution fusion | flops 9069926400 | bytes 10881540 | tf_op jit(solution)/shard_map/dot_general | solution.py:31
  443.0 11.5 %all-gather.9.cloned.1.call-done = f32[4,186,512]{2,1,0:T(8,128)} async-done(((f32[1,186,512]{2,1,0:T(8,128)}), f32[4,186,512]{2,1,0:T(8,128)}) %all-gather.9.cloned.1.call-update) | async-done | bytes 1523728 | tf_op jit(solution)/shard_map/all_gather | solution.py:65
  456.9 3.9 fusion.12
  460.8 3.0 gather_fusion.1
  465.3 3.7 collective-permute-start.8
  472.9 4.7 collective-permute-done.9
  479.0 2.4 collective-permute-done.10
  482.3 65.0 %all-reduce = (f32[512]{0:T(512)S(1)}, f32[512]{0:T(512)S(1)}) all-reduce(f32[512]{0:T(512)S(1)} %get-tuple-element.59, f32[512]{0:T(512)S(1)} %get-tuple-element.58), channel_id=1, replica_groups=mesh['sub'=32,'crs'=4] {'sub','crs'}, use_global_device_ids=true, to_apply=%region_2.3 | all-reduce | flops 1024 | bytes 8192 | tf_op jit(solution)/shard_map/psum | solution.py:92
  549.3 2.5 mul.380
  551.7 4.8 fusion.28
  557.6 3.7 collective-permute-start.12
  565.4 4.7 collective-permute-done.13
  570.1 2.1 collective-permute-done.15
  572.3 2.7 collective-permute-done.14
  578.1 2.5 stack.111
  580.6 63.7 %psum.53 = f32[512]{0:T(512)S(1)} all-reduce(f32[512]{0:T(512)S(1)} %broadcast_multiply_fusion.3), channel_id=1, replica_groups=mesh['sub'=32,'crs'=4] {'sub','crs'}, use_global_device_ids=true, to_apply=%region_8.9 | all-reduce | flops 512 | bytes 4096 | tf_op jit(solution)/shard_map/psum | solution.py:92
  644.3 7.7 scatter_custom_fusion.1
  653.6 2.6 fusion.61
  656.5 145.6 %all-reduce.9.cloned.1.call-done = f32[744,512]{1,0:T(8,128)} async-done(((f32[744,512]{1,0:T(8,128)}), f32[744,512]{1,0:T(8,128)}) %all-reduce.9.cloned.1.call-update) | async-done | bytes 1523728 | tf_op jit(solution)/shard_map/psum | solution.py:61
  802.1 3.4 convolution_bitcast_fusion.1
  805.5 13.4 %fusion = f32[512,1215]{0,1:T(8,128)} fusion(f32[1215,512]{1,0:T(8,128)S(1)} %scatter_custom_fusion.1, f32[1,1215,1215]{2,0,1:T(1,128)} %param.8), kind=kOutput, calls=%fused_computation.5 | convolution fusion | flops 9069926400 | bytes 10881540 | tf_op jit(solution)/shard_map/dot_general | solution.py:31
  819.0 11.5 %all-gather.11.cloned.1.call-done = f32[4,186,512]{2,1,0:T(8,128)} async-done(((f32[1,186,512]{2,1,0:T(8,128)}), f32[4,186,512]{2,1,0:T(8,128)}) %all-gather.11.cloned.1.call-update) | async-done | bytes 1523728 | tf_op jit(solution)/shard_map/all_gather | solution.py:65
  832.9 3.9 fusion.13
  836.8 3.0 gather_fusion.2
  841.3 3.7 collective-permute-start.16
  848.9 4.7 collective-permute-done.17
  855.0 2.4 collective-permute-done.18
  858.7 65.0 %psum.55 = f32[512]{0:T(512)S(1)} all-reduce(f32[512]{0:T(512)S(1)} %broadcast_multiply_fusion.2), channel_id=1, replica_groups=mesh['sub'=32,'crs'=4] {'sub','crs'}, use_global_device_ids=true, to_apply=%region_12.13 | all-reduce | flops 512 | bytes 4096 | tf_op jit(solution)/shard_map/psum | solution.py:92
  (214 shorter events, 62.1 us)
Async XLA Ops:
  7.2 158.0 %copy-start = (f32[186,744]{1,0:T(8,128)S(1)}, f32[186,744]{1,0:T(8,128)}, u32[]{:S(2)}) copy-start(f32[186,744]{1,0:T(8,128)} %param.11) | copy-start | bytes 1660612
  7.2 158.0 %all-reduce.5.cloned.1.call-start = ((), (), s32[]{:S(2)}) async-start(), calls=%async_computation | async-start | bytes 3047424 | tf_op jit(solution)/shard_map/psum | solution.py:61
  13.1 155.6 %copy-start.62 = (s32[1,4,147]{2,1,0:T(4,128)S(1)}, s32[1,4,147]{2,1,0:T(4,128)}, u32[]{:S(2)}) copy-start(s32[1,4,147]{2,1,0:T(4,128)} %param.7) | copy-start | bytes 7060
  13.1 180.5 %all-gather.7.cloned.1.call-start = ((), (), s32[]{:S(2)}) async-start(), calls=%async_computation.3 | async-start | bytes 1966080 | tf_op jit(solution)/shard_map/all_gather | solution.py:65
  168.6 257.4 %all-reduce.7.cloned.1.call-start = ((), (), s32[]{:S(2)}) async-start(), calls=%async_computation.1 | async-start | bytes 3047424 | tf_op jit(solution)/shard_map/psum | solution.py:61
  213.6 9.8 %copy-start.63 = (f32[4]{0:T(128)S(1)}, f32[4]{0:T(128)}, u32[]{:S(2)}) copy-start(f32[4]{0:T(128)} %constant.101) | copy-start | bytes 52
  213.6 18.6 %copy-start.1 = (f32[588,512]{1,0:T(8,128)S(1)}, f32[588,512]{1,0:T(8,128)}, u32[]{:S(2)}) copy-start(f32[588,512]{1,0:T(8,128)} %gather_fusion) | copy-start | bytes 3612676
  216.0 7.9 collective-permute-start
  219.7 8.8 collective-permute-start.1
  221.7 8.3 collective-permute-start.3
  223.3 8.9 collective-permute-start.2
  223.5 14.0 %copy-start.60 = (f32[4]{0:T(128)}, f32[4]{0:T(128)S(1)}, u32[]{:S(2)}) copy-start(f32[4]{0:T(128)S(1)} %get-tuple-element.14) | copy-start | bytes 52
  243.3 9.4 %collective-permute-start.4 = (f32[1,147,512]{2,1,0:T(8,128)}, f32[1,147,512]{2,1,0:T(8,128)S(1)}, u32[]{:S(2)}, u32[]{:S(2)}) collective-permute-start(f32[1,147,512]{2,1,0:T(8,128)} %get-tuple-element.46), channel_id=1, source_target_pairs={{0,4},{4,8},{8,12},{12,16},{16,20},{20,24},{24,28},{28,32},{32,36}... | collective-permute-start | bytes 903176 | tf_op jit(solution)/shard_map/ppermute | solution.py:17
  248.6 8.4 collective-permute-start.5
  250.5 6.5 collective-permute-start.7
  251.2 7.4 collective-permute-start.6
  275.6 178.8 %all-gather.9.cloned.1.call-start = ((), (), s32[]{:S(2)}) async-start(), calls=%async_computation.4 | async-start | bytes 1966080 | tf_op jit(solution)/shard_map/all_gather | solution.py:65
  429.5 372.6 %all-reduce.9.cloned.1.call-start = ((), (), s32[]{:S(2)}) async-start(), calls=%async_computation.2 | async-start | bytes 3047424 | tf_op jit(solution)/shard_map/psum | solution.py:61
  463.8 17.6 %copy-start.3 = (f32[588,512]{1,0:T(8,128)S(1)}, f32[588,512]{1,0:T(8,128)}, u32[]{:S(2)}) copy-start(f32[588,512]{1,0:T(8,128)} %gather_fusion.1) | copy-start | bytes 3612676
  465.3 7.6 collective-permute-start.8
  469.1 8.5 collective-permute-start.9
  471.0 8.0 collective-permute-start.11
  472.4 9.3 copy-start.29
  472.4 8.9 collective-permute-start.10
  481.6 66.2 %copy-start.16 = (f32[1,147,512]{2,1,0:T(8,128)}, f32[1,147,512]{2,1,0:T(8,128)S(1)}, u32[]{:S(2)}) copy-start(f32[1,147,512]{2,1,0:T(8,128)S(1)} %get-tuple-element.35) | copy-start | bytes 903172
  481.6 66.2 %copy-start.19 = (f32[1,147,512]{2,1,0:T(8,128)}, f32[1,147,512]{2,1,0:T(8,128)S(1)}, u32[]{:S(2)}) copy-start(f32[1,147,512]{2,1,0:T(8,128)S(1)} %get-tuple-element.36) | copy-start | bytes 903172
  481.6 66.2 %copy-start.22 = (f32[1,147,512]{2,1,0:T(8,128)}, f32[1,147,512]{2,1,0:T(8,128)S(1)}, u32[]{:S(2)}) copy-start(f32[1,147,512]{2,1,0:T(8,128)S(1)} %get-tuple-element.37) | copy-start | bytes 903172
  481.6 94.9 %copy-start.14 = (f32[1,147,512]{2,1,0:T(8,128)}, f32[1,147,512]{2,1,0:T(8,128)S(1)}, u32[]{:S(2)}) copy-start(f32[1,147,512]{2,1,0:T(8,128)S(1)} %get-tuple-element.34) | copy-start | bytes 903172
  481.7 66.1 %copy-start.61 = (f32[4]{0:T(128)S(1)}, f32[4]{0:T(128)}, u32[]{:S(2)}) copy-start(f32[4]{0:T(128)} %copy-done.60) | copy-start | bytes 52
  557.6 7.8 collective-permute-start.12
  561.3 8.8 collective-permute-start.13
  563.2 9.0 collective-permute-start.15
  564.2 10.8 %collective-permute-start.14 = (f32[1,147,512]{2,1,0:T(8,128)}, f32[1,147,512]{2,1,0:T(8,128)}, u32[]{:S(2)}, u32[]{:S(2)}) collective-permute-start(f32[1,147,512]{2,1,0:T(8,128)} %get-tuple-element.33), channel_id=1, source_target_pairs={{0,1},{1,2},{2,3},{3,0},{4,5},{5,6},{6,7},{7,4},{8,9},{9,10},{10,1... | collective-permute-start | bytes 903176 | tf_op jit(solution)/shard_map/ppermute | solution.py:17
  564.9 11.7 %copy-start.17 = (f32[1,147,512]{2,1,0:T(8,128)S(1)}, f32[1,147,512]{2,1,0:T(8,128)}, u32[]{:S(2)}) copy-start(f32[1,147,512]{2,1,0:T(8,128)} %copy-done.16) | copy-start | bytes 903172
  564.9 11.7 %copy-start.20 = (f32[1,147,512]{2,1,0:T(8,128)S(1)}, f32[1,147,512]{2,1,0:T(8,128)}, u32[]{:S(2)}) copy-start(f32[1,147,512]{2,1,0:T(8,128)} %copy-done.19) | copy-start | bytes 903172
  564.9 11.7 %copy-start.23 = (f32[1,147,512]{2,1,0:T(8,128)S(1)}, f32[1,147,512]{2,1,0:T(8,128)}, u32[]{:S(2)}) copy-start(f32[1,147,512]{2,1,0:T(8,128)} %copy-done.22) | copy-start | bytes 903172
  656.2 174.3 %all-gather.11.cloned.1.call-start = ((), (), s32[]{:S(2)}) async-start(), calls=%async_computation.5 | async-start | bytes 1966080 | tf_op jit(solution)/shard_map/all_gather | solution.py:65
  839.8 17.5 %copy-start.2 = (f32[588,512]{1,0:T(8,128)S(1)}, f32[588,512]{1,0:T(8,128)}, u32[]{:S(2)}) copy-start(f32[588,512]{1,0:T(8,128)} %gather_fusion.2) | copy-start | bytes 3612676
  841.3 7.6 collective-permute-start.16
  845.1 8.5 collective-permute-start.17
  847.0 8.0 collective-permute-start.19
  848.4 9.3 copy-start.36
  848.4 9.3 copy-start.38
  848.4 9.3 copy-start.40
  848.4 9.3 copy-start.42
  848.5 9.3 copy-start.44
  848.5 8.9 collective-permute-start.18
  857.7 66.0 %copy-start.59 = (f32[512]{0:T(512)S(1)}, f32[512]{0:T(512)}, u32[]{:S(2)}) copy-start(f32[512]{0:T(512)} %get-tuple-element.12) | copy-start | bytes 6148
  (43 other events, 144.3 us)
Sparse Core Ops, SparseCore 0:
  13.2 151.9 all-reduce.4
  168.7 24.7 all-gather.6
  275.7 150.2 all-reduce.6
  429.6 24.7 all-gather.8
  656.3 145.7 all-reduce.8
  805.6 24.7 all-gather.10
where the time goes:
time: 945 us; the launch traced here: 936 us
  waiting for transfers between devices  536 us (57%)
  blocking collectives  194 us (21%)
  matrix products  85.7 us (9%)
  starting transfers between devices  38.7 us (4%)
  local copies, waits for them, and re-layouts  38 us (4%)
  other arithmetic  28.5 us (3%)
  between operations  15.4 us (2%)
    psum x3, waiting for transfers between devices, assemble(): return lax.psum(tdot(emap, partial_value), ('sub', 'crs'))  448 us
    psum x3, blocking collectives, inner(): return lax.psum(0.5 * jnp.sum(left * right, axis=(0, 1)), ('sub', 'crs'))  194 us
    dot_general x14, matrix products, hdot(): return jnp.dot(left, right, precision=lax.Precision.HIGHEST)  71.5 us
    all_gather x3, waiting for transfers between devices, coarse(): lax.all_gather(hdot(coarse_inverse, total), 'crs', axis=0, tiled=True)  47.7 us
    ppermute x10, waiting for transfers between devices, padded(): lax.ppermute(head, axis, [((i + 1) % count, i) for i in range(ends)])  29.3 us
    ppermute x10, starting transfers between devices, padded(): lax.ppermute(tail, axis, [(i, (i + 1) % count) for i in range(ends)])  22 us
  transfers between devices with their start and end apart: 26, of which 25 were waited for; matrix products, arithmetic and copies ran while one was open for 3% of the time, Pallas kernels for 0%

commit v1 on v0

v1 whole, which is shorter than its diff:
```python
import functools

import jax
import jax.numpy as jnp
from jax import lax
from jax.experimental import pallas as pl
from jax.experimental.pallas import tpu as pltpu
from jax.sharding import PartitionSpec as P

F32 = jnp.float32
BF16 = jnp.bfloat16
MESH = pl.DeviceIdType.MESH

FACE = 160
SENT = 152
NX = 4 * FACE
NA = NX + 32
ORDER = (2, 3, 0, 1)
LANES = 128


def dot(left, right):
    return jnp.dot(left, right, preferred_element_type=F32)


def dot_nt(left, right):
    return lax.dot_general(left, right, (((1,), (1,)), ((), ())), preferred_element_type=F32)


def split(value):
    high = value.astype(BF16)
    return high, (value - high.astype(F32)).astype(BF16)


def hot(cond, value=1.0):
    return jnp.where(cond, value, 0.0).astype(BF16)


def rows_of(shape):
    return lax.broadcasted_iota(jnp.int32, shape, 0)


def cols_of(shape):
    return lax.broadcasted_iota(jnp.int32, shape, 1)


def div(value, by):
    return (value * (65536 // by + 1)) >> 16


def kernel(dims, idxc, idxr, kinv, schur, corner, cinv, loads, mo, ro,
           kv, lv, cv, sv, civ, khi, klo, tail, bmat, bmt, a0hi, a0lo, lhi, llo, a3, m3, w3, x3,
           cpad, chi, clo, cip, sp, tmat, tmt, ws, wo, wr, dall, dphi, dplo,
           tb, rb, rv, dv, pbuf, p0, p1, gb, sibs, sibr, hk, hb, h3,
           rs, rr, es, er, fr,
           dsem, fsend, frecv, wsend, wrecv, csend, crecv,
           s1as, s1ar, s1bs, s1br, s2s, s2r, bs, br, s3s, s3r,
           r1s, r1r, r2s, r2r, r3s, r3r):
    nsub, ncrs, nrows, fdof, cases, ncoarse = dims
    chips = nsub // 2
    nrp = khi.shape[1]
    cblock = ncoarse // ncrs
    cbp, ncp = cip.shape
    a = lax.axis_index("sub")
    b = lax.axis_index("crs")
    k = lax.div(a, 2)
    c = lax.rem(a, 2)
    sib = 2 * k + 1 - c
    up = lax.rem(a + 1, nsub)
    down = lax.rem(a + nsub - 1, nsub)
    left = lax.rem(b + ncrs - 1, ncrs)
    right = lax.rem(b + 1, ncrs)
    dests = ((a, left), (a, right), (down, b), (up, b))
    keeps = (None, None, a > 0, a < nsub - 1)
    drains = []

    def local(src, dst, n):
        return pltpu.make_async_copy(src, dst, dsem.at[n])

    def remote(src, dst, ssem, rsem, dev):
        return pltpu.make_async_remote_copy(
            src_ref=src, dst_ref=dst, send_sem=ssem, recv_sem=rsem, device_id=dev, device_id_type=MESH)

    def settle(ref, sem):
        pltpu.make_async_copy(ref, ref, sem).wait()

    in_copies = [local(corner.at[0], cv, 0), local(cinv, civ, 1), local(loads.at[0], lv, 2),
                 local(kinv.at[0], kv, 3), local(schur.at[0], sv, 4)]
    for copy in in_copies:
        copy.start()

    barrier = pltpu.get_barrier_semaphore()
    for j in range(1, ncrs):
        pl.semaphore_signal(barrier, inc=1, device_id=(a, lax.rem(b + j, ncrs)), device_id_type=MESH)
    for j in range(ncrs):
        pl.semaphore_signal(barrier, inc=1, device_id=(up, j), device_id_type=MESH)
        pl.semaphore_signal(barrier, inc=1, device_id=(down, j), device_id_type=MESH)

    def greet(j, carry):
        pl.semaphore_signal(barrier, inc=1, device_id=(2 * lax.rem(k + j, chips) + c, b), device_id_type=MESH)
        return carry

    lax.fori_loop(1, chips, greet, 0)

    for pos in range(4):
        sign = 1.0 if pos % 2 else -1.0
        band = slice(pos * FACE, (pos + 1) * FACE)
        bmat[band, :] = hot(idxc[band, :] == cols_of((FACE, nrp)), sign)
    lane = cols_of((1, NX))
    signs = jnp.where(((lane >= FACE) & (lane < 2 * FACE)) | (lane >= 3 * FACE), 1.0, -1.0)

    def build_bmt(i, carry):
        at = pl.multiple_of(i * LANES, LANES)
        rows = rows_of((LANES, NX)) + at
        bmt[pl.ds(at, LANES), :] = jnp.where(idxr[...] == rows, signs, 0.0).astype(BF16)
        return carry

    lax.fori_loop(0, nrp // LANES, build_bmt, 0)

    for n in range(2):
        for pos in range(4):
            rb[n, pos, SENT:FACE, :] = jnp.zeros((FACE - SENT, cases), F32)
    hb[:, 96:LANES, :] = jnp.zeros((3, 32, cases), F32)
    cpad[...] = jnp.zeros(cpad.shape, F32)
    cip[...] = jnp.zeros(cip.shape, F32)
    sp[...] = jnp.zeros(sp.shape, F32)
    edge = nrp - LANES
    khi[:, edge:] = jnp.zeros((nrp, LANES), BF16)
    klo[:, edge:] = jnp.zeros((nrp, LANES), BF16)
    whole = nrows // 16 * 16
    for ref in (khi, klo, lhi, llo):
        ref[whole:, :] = jnp.zeros((nrp - whole, ref.shape[1]), BF16)
    tail[...] = jnp.zeros(tail.shape, F32)

    in_copies[0].wait()
    ncl = cv.shape[1]
    cpad[0:nrows, 0:ncl] = cv[...]
    high, low = split(cpad[...])
    chi[...] = high
    clo[...] = low
    w = rows_of((32, 1))
    pick_l = jnp.where(w < 12, w, jnp.where((w >= 16) & (w < 28), w - 4, -1))
    sel = hot(pick_l == cols_of((32, LANES)))
    a0hi[0:32, :] = dot_nt(sel, chi[...]).astype(BF16)
    a0lo[0:32, :] = dot_nt(sel, clo[...]).astype(BF16)
    bch = dot(bmat[...], chi[...]).astype(BF16)
    bcl = dot(bmat[...], clo[...]).astype(BF16)
    l = rows_of((LANES, 1))
    da = div(l, 12)
    rem12 = l - 12 * da
    db = div(rem12, 6)
    where_l = 24 * (1 + da) + 6 * lax.rem(b + db, ncrs) + rem12 - 6 * db
    where_l = jnp.where(l < 24, where_l, -1000)
    lanes = cols_of((LANES, LANES))
    emaps = [hot(where_l + off == lanes) for off in (0, 24, -24)]
    wo[...] = dot(bch, emaps[0]) + dot(bcl, emaps[0])
    ws[0:2 * FACE, :] = wo[0:2 * FACE, :]
    for pos in (2, 3):
        band = slice(pos * FACE, (pos + 1) * FACE)
        ws[band, :] = dot(bch[band], emaps[pos - 1]) + dot(bcl[band], emaps[pos - 1])
    pl.semaphore_wait(barrier, ncrs - 1 + 2 * ncrs + chips - 1)
    wcopies = [remote(ws.at[pl.ds(pos * FACE, FACE)], wr.at[pl.ds((pos ^ 1) * FACE, FACE)],
                      wsend.at[pos], wrecv.at[pos ^ 1], dests[pos]) for pos in range(4)]
    for copy in wcopies:
        copy.start()

    in_copies[1].wait()
    cip[0:cblock, 0:ncoarse] = civ[...]
    high, low = split(cip[...])
    i = cols_of((1, cbp))
    r = cblock * b + i
    plane = div(r, 24)
    base = lax.div(lax.div(cblock * b, 24), 2)
    target = 24 * ((plane >> 1) - base) + r - 24 * plane
    target = jnp.where((((plane + 1) & 1) == c) & (i < cblock), target, -1)
    pct = hot(target == rows_of((LANES, cbp)))
    x1h = dot(pct, high).astype(BF16)
    x1l = dot(pct, low).astype(BF16)
    i = rows_of((LANES, 1))
    r = 48 * k - 48 + i
    r = jnp.where((i < 120) & (r < ncoarse), r, -1)
    sel = hot(r == cols_of((LANES, ncp)))
    dall[b] = dot_nt(sel, x1h) + dot_nt(sel, x1l)
    for j in range(1, ncrs):
        remote(dall.at[b], dall.at[b], csend.at[j], crecv.at[j], (a, lax.rem(b + j, ncrs))).start()

    in_copies[2].wait()
    step = 16 * 5

    def split_loads(i, carry):
        at = pl.multiple_of(i * step, step)
        high, low = split(lv[pl.ds(at, step), :])
        lhi[pl.ds(at, step), :] = high
        llo[pl.ds(at, step), :] = low
        return carry

    lax.fori_loop(0, whole // step, split_loads, 0)
    left_rows = nrows - whole
    tail[0:left_rows, 0:cases] = lv[whole:nrows, :]
    high, low = split(tail[:, 0:cases])
    lhi[whole:whole + 16, :] = high
    llo[whole:whole + 16, :] = low

    def apply_loads(lo, hi):
        high, low = a0hi[lo:hi, :], a0lo[lo:hi, :]
        return dot(high, lhi[...]) + dot(high, llo[...]) + dot(low, lhi[...])

    t = cols_of((1, LANES))
    blk = jnp.where(t >= 64, t - 64, t)
    src_b = blk >> 4
    w = blk & 15
    db = jnp.where(w >= 6, 1, 0)
    plane_row = jnp.where(w < 12, 6 * ((src_b + db) & (ncrs - 1)) + w - 6 * db, -1)
    gather_hot = hot(plane_row == rows_of((32, LANES)))

    def coarse_begin(f):
        for j in range(1, ncrs):
            to = lax.rem(b + j, ncrs)
            at = pl.ds(pl.multiple_of(to * LANES, LANES), LANES)
            remote(pbuf.at[f, pl.ds(0, 16), at], p0.at[f, b], s1as.at[f], s1ar.at[f], (a, to)).start()
        for j in range(ncrs):
            to = lax.rem(b + j, ncrs)
            at = pl.ds(pl.multiple_of(to * LANES, LANES), LANES)
            remote(pbuf.at[f, pl.ds(16, 16), at], p1.at[f, b], s1bs.at[f], s1br.at[f], (up, to)).start()
        at = pl.ds(pl.multiple_of(b * LANES, LANES), LANES)
        p0[f, b] = pbuf[f, 0:16, at]

        def drain():
            settle(p0.at[f, pl.ds(0, ncrs - 1)], s1as.at[f])
            settle(p1.at[f], s1bs.at[f])

        drains.append(drain)

    def coarse_gather(f):
        settle(p0.at[f, pl.ds(0, ncrs - 1)], s1ar.at[f])
        settle(p1.at[f], s1br.at[f])
        pieces = jnp.concatenate([p0[f].reshape(16 * ncrs, LANES), p1[f].reshape(16 * ncrs, LANES)], axis=0)
        high, low = split(pieces)
        gb[f, k] = (dot(gather_hot, high) + dot(gather_hot, low))[0:24]

        def send(j, carry):
            to = 2 * lax.rem(k + j, chips) + c
            remote(gb.at[f, k], gb.at[f, k], s2s.at[f], s2r.at[f], (to, b)).start()
            return carry

        lax.fori_loop(1, chips, send, 0)
        drains.append(lambda: settle(gb.at[f, pl.ds(0, chips - 1)], s2s.at[f]))

    def coarse_solve(f):
        settle(gb.at[f, pl.ds(0, chips - 1)], s2r.at[f])
        high, low = split(gb[f].reshape(chips * 24, LANES))
        sibs[f, 0:LANES] = dot(dphi[...], high) + dot(dphi[...], low) + dot(dplo[...], high)
        sibs[f, LANES:LANES + 24] = gb[f, k]
        copy = remote(sibs.at[f], sibr.at[f], bs.at[f], br.at[f], (sib, b))
        copy.start()
        return copy

    def coarse_spread(f, copy):
        copy.wait()
        hk[...] = sibs[f, 0:LANES] + sibr[f, 0:LANES]
        at = pl.ds(pl.multiple_of(b * LANES, LANES), LANES)
        hb[f, 0:96, at] = hk[pl.ds(pl.multiple_of(24 * c, 8), 96), :]
        for j in range(1, ncrs):
            remote(hb.at[f, pl.ds(0, 96), at], hb.at[f, pl.ds(0, 96), at], s3s.at[f], s3r.at[f],
                   (a, lax.rem(b + j, ncrs))).start()
        drains.append(lambda: settle(hb.at[f, pl.ds(0, 96), pl.ds(0, (ncrs - 1) * LANES)], s3s.at[f]))
        mine = hk[pl.ds(pl.multiple_of(24 + 24 * c, 8), 24), :] * sibs[f, LANES:LANES + 24]
        other = hk[pl.ds(pl.multiple_of(48 - 24 * c, 8), 24), :] * sibr[f, LANES:LANES + 24]
        return jnp.sum(mine + other, axis=0, keepdims=True)

    def coarse_end(f):
        settle(hb.at[f, pl.ds(0, 96), pl.ds(0, (ncrs - 1) * LANES)], s3r.at[f])
        high, low = split(hb[f])
        h3[0:LANES, :] = high
        h3[LANES:2 * LANES, :] = low
        h3[2 * LANES:, :] = high

    def sum_begin(n):
        for cc in range(2):
            for j in range(ncrs):
                to = lax.rem(b + j, ncrs)
                at = pl.ds(pl.multiple_of(to * LANES, LANES), LANES)
                if cc == 0 and j == 0:
                    rr[n, c * ncrs + b] = rs[n, :, at]
                    continue
                dev = (a if cc == 0 else sib, to)
                remote(rs.at[n, :, at], rr.at[n, c * ncrs + b], r1s.at[n], r1r.at[n], dev).start()
        drains.append(lambda: settle(rr.at[n, pl.ds(0, 2 * ncrs - 1)], r1s.at[n]))

    def sum_chip(n):
        settle(rr.at[n, pl.ds(0, 2 * ncrs - 1)], r1r.at[n])
        return jnp.sum(rr[n], axis=0)

    def sum_gather(n, block):
        er[n, k] = block

        def send(j, carry):
            to = 2 * lax.rem(k + j, chips) + c
            remote(er.at[n, k], er.at[n, k], r2s.at[n], r2r.at[n], (to, b)).start()
            return carry

        lax.fori_loop(1, chips, send, 0)
        drains.append(lambda: settle(er.at[n, pl.ds(0, chips - 1)], r2s.at[n]))

    def sum_spread(n):
        settle(er.at[n, pl.ds(0, chips - 1)], r2r.at[n])
        at = pl.ds(pl.multiple_of(b * LANES, LANES), LANES)
        fr[n, :, at] = jnp.sum(er[n], axis=0)
        for j in range(1, ncrs):
            remote(fr.at[n, :, at], fr.at[n, :, at], r3s.at[n], r3r.at[n], (a, lax.rem(b + j, ncrs))).start()
        drains.append(lambda: settle(fr.at[n, :, pl.ds(0, (ncrs - 1) * LANES)], r3s.at[n]))

    def sum_end(n):
        settle(fr.at[n, :, pl.ds(0, (ncrs - 1) * LANES)], r3r.at[n])
        return fr[n, 0:1, :], fr[n, 1:2, :]

    def faces_start(n, which):
        copies = []
        for pos in which:
            copy = remote(tb.at[n % 2, pl.ds(pos * FACE, SENT)], rb.at[n % 2, pos ^ 1, pl.ds(0, SENT)],
                          fsend.at[n % 2, pos], frecv.at[n % 2, pos ^ 1], dests[pos])
            copy.start()
            copies.append(copy)
        return copies

    def faces_wait(copies):
        for copy in copies:
            copy.wait()

    def jumped(n, pos, extra=None):
        band = slice(pos * FACE, (pos + 1) * FACE)
        value = tb[n % 2, band, :] + rb[n % 2, pos]
        if extra is not None:
            value = value + extra
        if keeps[pos] is not None:
            value = jnp.where(keeps[pos], value, 0.0)
        return value

    def put_x(pos, value):
        high, low = split(value)
        lo = pos * FACE
        x3[lo:lo + FACE, :] = high
        x3[NX + lo:NX + lo + FACE, :] = low
        x3[2 * NX + lo:2 * NX + lo + FACE, :] = high

    pbuf[0] = apply_loads(0, 32)
    coarse_begin(0)
    in_copies[3].wait()

    def split_k(i, carry):
        at = pl.multiple_of(i * step, step)
        high, low = split(kv[pl.ds(at, step), :])
        khi[pl.ds(at, step), 0:nrows] = high
        klo[pl.ds(at, step), 0:nrows] = low
        return carry

    lax.fori_loop(0, whole // step, split_k, 0)
    tail[0:left_rows, 0:nrows] = kv[whole:nrows, :]
    high, low = split(tail[...])
    khi[whole:whole + 16, :] = high
    klo[whole:whole + 16, :] = low

    def face_rows(lo, hi):
        def tile(i, carry):
            at = pl.ds(pl.multiple_of(i * 256, 256), 256)
            a0hi[32 + lo:32 + hi, at] = dot(bmat[lo:hi, :], khi[:, at]).astype(BF16)
            a0lo[32 + lo:32 + hi, at] = dot(bmat[lo:hi, :], klo[:, at]).astype(BF16)
            return carry

        lax.fori_loop(0, nrp // 256, tile, 0)

    half = 2 * FACE
    face_rows(0, half)
    tb[0, 0:half, :] = apply_loads(32, 32 + half)
    copies = faces_start(0, (0, 1))
    coarse_gather(0)
    face_rows(half, NX)
    tb[0, half:NX, :] = apply_loads(32 + half, 32 + NX)
    copies += faces_start(0, (2, 3))

    for j in range(1, ncrs):
        copy = remote(dall.at[b], dall.at[b], csend.at[j], crecv.at[j], (a, lax.rem(b + j, ncrs)))
        copy.wait()
    total_hi = total_lo = None
    for blk_b in range(ncrs):
        j = rows_of((LANES, 1))
        pair = div(j, 24)
        rem = j - 24 * pair
        pair = pair + (cblock * blk_b // 24) // 2
        r = 24 * (2 * pair + 1 - c) + rem
        target = jnp.where((j < 120) & (r >= cblock * blk_b) & (r < cblock * (blk_b + 1)),
                           24 * (pair + 1 - c) + rem, -1)
        perm = hot(target == cols_of((LANES, chips * 24)))
        high, low = split(dall[blk_b])
        ph, plo = dot(high, perm), dot(low, perm)
        total_hi = ph if total_hi is None else total_hi + ph
        total_lo = plo if total_lo is None else total_lo + plo
    dphi[...] = total_hi.astype(BF16)
    dplo[...] = total_lo.astype(BF16)

    coarse_copy = coarse_solve(0)

    def between(i, carry):
        at = pl.multiple_of(i * 224, 16)
        high = dot(a0hi[pl.ds(at, 224), :], bmt[...]).astype(BF16)
        a3[pl.ds(at, 224), 0:NX] = high
        a3[pl.ds(at, 224), NX:2 * NX] = high
        a3[pl.ds(at, 224), 2 * NX:] = dot(a0lo[pl.ds(at, 224), :], bmt[...]).astype(BF16)
        return carry

    lax.fori_loop(0, NA // 224, between, 0)
    coarse_spread(0, coarse_copy)

    in_copies[4].wait()
    nface = sv.shape[0]
    sp[0:nface, 0:nface] = sv[...]
    high, low = split(sp[...])
    khi[0:NX, 0:NX] = high
    klo[0:NX, 0:NX] = low
    for pos in range(4):
        face = ORDER[pos]
        sign = 0.5 if pos % 2 else -0.5
        j = rows_of((FACE, 1))
        target = jnp.where(j < fdof, j + face * fdof, -1)
        tmat[pos * FACE:(pos + 1) * FACE, :] = hot(target == cols_of((FACE, NX)), sign)
    pos_l = jnp.where(lane >= FACE, 1, 0) + jnp.where(lane >= 2 * FACE, 1, 0) + jnp.where(lane >= 3 * FACE, 1, 0)
    j = lane - FACE * pos_l
    target = jnp.where(j < fdof, j + fdof * ((pos_l + 2) & 3), -1)
    kept = jnp.where(pos_l == 2, jnp.where(a > 0, 0.5, 0.0), jnp.where(pos_l == 3, jnp.where(a < nsub - 1, 0.5, 0.0), 0.5))
    tmt[...] = jnp.where(target == rows_of((NX, NX)), signs * kept, 0.0).astype(BF16)

    def precond_rows(i, carry):
        at = pl.ds(pl.multiple_of(i * FACE, FACE), FACE)
        high = dot(tmat[at, :], khi[0:NX, 0:NX]).astype(BF16)
        low = dot(tmat[at, :], klo[0:NX, 0:NX]).astype(BF16)
        high = dot(high, tmt[...]).astype(BF16)
        m3[at, 0:NX] = high
        m3[at, NX:2 * NX] = high
        m3[at, 2 * NX:] = dot(low, tmt[...]).astype(BF16)
        return carry

    lax.fori_loop(0, 4, precond_rows, 0)

    for copy in wcopies:
        copy.wait()
    high, low = split(wo[...] + wr[...])
    w3[:, 0:LANES] = high
    w3[:, LANES:2 * LANES] = high
    w3[:, 2 * LANES:] = low

    def operator_end(n, f, copies, use):
        coarse_end(f)
        faces_wait(copies)
        for pos in range(4):
            use(pos, jumped(n, pos, dot(w3[pos * FACE:(pos + 1) * FACE, :], h3[...])))

    def first_use(pos, value):
        rv[pos * FACE:(pos + 1) * FACE, :] = value
        put_x(pos, value)

    operator_end(0, 0, copies, first_use)

    def precond(n):
        tb[n % 2, 0:half, :] = dot(m3[0:half, :], x3[...])
        copies = faces_start(n, (0, 1))
        tb[n % 2, half:, :] = dot(m3[half:, :], x3[...])
        copies += faces_start(n, (2, 3))
        return copies, jnp.sum(rv[...] * tb[n % 2], axis=0, keepdims=True)

    row8 = rows_of((8, cases))

    def operator(n, f, extra):
        block = dot(a3[0:32 + half, :], x3[...])
        pbuf[f] = block[0:32]
        coarse_begin(f)
        tb[n % 2, 0:half, :] = block[32:]
        copies = faces_start(n, (0, 1))
        tb[n % 2, half:, :] = dot(a3[32 + half:, :], x3[...])
        copies += faces_start(n, (2, 3))
        energy = jnp.sum(dv[...] * tb[n % 2], axis=0, keepdims=True)
        rs[f] = jnp.where(row8 == 0, extra, jnp.where(row8 == 1, energy, 0.0))
        sum_begin(f)
        coarse_gather(f)
        block = sum_chip(f)
        copy = coarse_solve(f)
        ce = coarse_spread(f, copy)
        sum_gather(f, block + jnp.where(rows_of((8, LANES)) == 1, ce, 0.0))
        return copies

    copies, rz_part = precond(1)
    faces_wait(copies)
    for pos in range(4):
        value = jumped(1, pos)
        dv[pos * FACE:(pos + 1) * FACE, :] = value
        put_x(pos, value)

    copies = operator(2, 1, rz_part)

    def keep_image(n):
        def use(pos, value):
            tb[n % 2, pos * FACE:(pos + 1) * FACE, :] = value
        return use

    operator_end(2, 1, copies, keep_image(2))
    sum_spread(1)
    rz_now, energy = sum_end(1)
    alpha = rz_now / energy
    for pos in range(4):
        band = slice(pos * FACE, (pos + 1) * FACE)
        value = rv[band, :] - alpha * tb[0, band, :]
        rv[band, :] = value
        put_x(pos, value)
        mo[0, ORDER[pos]] = (alpha * dv[band, :])[0:fdof]

    copies, rz_part = precond(3)
    rs[0] = jnp.where(row8 == 0, rz_part, 0.0)
    sum_begin(0)
    sum_gather(0, sum_chip(0))
    sum_spread(0)
    rz_next, _ = sum_end(0)
    beta = rz_next / rz_now
    faces_wait(copies)
    for pos in range(4):
        band = slice(pos * FACE, (pos + 1) * FACE)
        value = jumped(3, pos) + beta * dv[band, :]
        dv[band, :] = value
        put_x(pos, value)

    copies = operator(4, 2, rz_part)
    operator_end(4, 2, copies, keep_image(4))
    sum_spread(2)
    _, energy = sum_end(2)
    alpha = rz_next / energy
    for pos in range(4):
        band = slice(pos * FACE, (pos + 1) * FACE)
        ro[0, ORDER[pos]] = (rv[band, :] - alpha * tb[0, band, :])[0:fdof]
        mo[0, ORDER[pos]] = mo[0, ORDER[pos]] + (alpha * dv[band, :])[0:fdof]

    for drain in drains:
        drain()


def body(face_index, kinv, schur, corner, coarse_inverse, loads):
    nsub = lax.axis_size("sub")
    ncrs = lax.axis_size("crs")
    fdof = face_index.shape[2]
    nrows, cases = loads.shape[1:]
    ncoarse = coarse_inverse.shape[1]
    nface = schur.shape[1]
    ncl = corner.shape[2]
    chips = nsub // 2
    nrp = -(-nrows // 256) * 256
    cbp = -(-coarse_inverse.shape[0] // 16) * 16
    ncp = -(-ncoarse // LANES) * LANES
    idx = jnp.pad(face_index[0], ((0, 0), (0, FACE - fdof)), constant_values=-1)
    idx = jnp.concatenate([idx[2:4], idx[0:2]], axis=0)
    vm = pltpu.VMEM
    dma = pltpu.SemaphoreType.DMA
    scratch = [
        vm((nrows, nrows), F32), vm((nrows, cases), F32), vm((nrows, ncl), F32), vm((nface, nface), F32),
        vm(coarse_inverse.shape, F32),
        vm((nrp, nrp), BF16), vm((nrp, nrp), BF16), vm((16, nrp), F32),
        vm((NX, nrp), BF16), vm((nrp, NX), BF16), vm((NA, nrp), BF16), vm((NA, nrp), BF16),
        vm((nrp, cases), BF16), vm((nrp, cases), BF16),
        vm((NA, 3 * NX), BF16), vm((NX, 3 * NX), BF16), vm((NX, 3 * LANES), BF16), vm((3 * NX, cases), BF16),
        vm((nrp, LANES), F32), vm((nrp, LANES), BF16), vm((nrp, LANES), BF16), vm((cbp, ncp), F32),
        vm((NX, NX), F32), vm((NX, NX), BF16), vm((NX, NX), BF16),
        vm((NX, LANES), F32), vm((NX, LANES), F32), vm((NX, LANES), F32),
        vm((ncrs, LANES, LANES), F32), vm((LANES, chips * 24), BF16), vm((LANES, chips * 24), BF16),
        vm((2, NX, cases), F32), vm((2, 4, FACE, cases), F32), vm((NX, cases), F32), vm((NX, cases), F32),
        vm((3, 32, cases), F32), vm((3, ncrs, 16, LANES), F32), vm((3, ncrs, 16, LANES), F32),
        vm((3, chips, 24, LANES), F32),
        vm((3, LANES + 24, LANES), F32), vm((3, LANES + 24, LANES), F32), vm((LANES, LANES), F32),
        vm((3, LANES, cases), F32), vm((3 * LANES, cases), BF16),
        vm((3, 8, cases), F32), vm((3, 2 * ncrs, 8, LANES), F32), vm((3, 8, LANES), F32),
        vm((3, chips, 8, LANES), F32), vm((3, 8, cases), F32),
        dma((5,)), dma((2, 4)), dma((2, 4)), dma((4,)), dma((4,)), dma((ncrs,)), dma((ncrs,)),
    ] + [dma((3,)) for _ in range(16)]
    out = jax.ShapeDtypeStruct((1, 4, fdof, cases), F32)
    anyspace = pl.BlockSpec(memory_space=pl.ANY)
    inside = pl.BlockSpec(memory_space=pltpu.VMEM)
    dims = (nsub, ncrs, nrows, fdof, cases, ncoarse)
    return pl.pallas_call(
        functools.partial(kernel, dims),
        out_shape=(out, out),
        in_specs=[inside, inside] + [anyspace] * 5,
        out_specs=(inside, inside),
        scratch_shapes=scratch,
        compiler_params=pltpu.CompilerParams(
            collective_id=0, has_side_effects=True, vmem_limit_bytes=63 * 2**20),
    )(idx.reshape(NX, 1), idx.reshape(1, NX), kinv, schur, corner, coarse_inverse, loads)


def solution(mesh):
    subs = P(("sub", "crs"), None, None)
    out = P(("sub", "crs"), None, None, None)
    return jax.shard_map(
        body, mesh=mesh, in_specs=(subs, subs, subs, subs, P("crs", None), subs), out_specs=(out, out),
        check_vma=False)
```

time: 945 us -> 121 us (0.13)
  waiting for transfers between devices: 536 us -> 0 us
  blocking collectives: 194 us -> 0 us
  Pallas kernels: 0 us -> 103 us
  matrix products: 85.7 us -> 0 us
  starting transfers between devices: 38.7 us -> 0 us
  other arithmetic: 28.5 us -> 0.01 us
  local copies, waits for them, and re-layouts: 38 us -> 17.1 us
  between operations: 15.4 us -> 0.65 us
    psum x3 -> x0, waiting for transfers between devices: 448 us -> none  [assemble(): return lax.psum(tdot(emap, partial_value), ('sub', 'crs'))]
    psum x3 -> x0, blocking collectives: 194 us -> none  [inner(): return lax.psum(0.5 * jnp.sum(left * right, axis=(0, 1)), ('sub', 'crs'))]
    pallas_call x0 -> x1, Pallas kernels: none -> 103 us  [body(): pl.pallas_call(functools.partial(kernel, dims), out_shape=(out, out), in_...]
    dot_general x20 -> x0, matrix products: 85.7 us -> none  [the longest x14 71.5 us: hdot(): return jnp.dot(left, right, precision=lax.Precision.HIGHEST)]
    all_gather x3 -> x0, waiting for transfers between devices: 47.7 us -> none  [coarse(): lax.all_gather(hdot(coarse_inverse, total), 'crs', axis=0, tiled=True)]
    ppermute x20 -> x0, waiting for transfers between devices: 40.2 us -> none  [the longest x10 29.3 us: padded(): lax.ppermute(head, axis, [((i + 1) % count, i) for i in range(ends)])]
    ppermute x20 -> x0, starting transfers between devices: 37.8 us -> none  [the longest x10 22 us: padded(): lax.ppermute(tail, axis, [(i, (i + 1) % count) for i in range(ends)])]
    scatter x2 -> x0, other arithmetic: 15 us -> none  [body(): image = operator(jnp.zeros((nrows, cases), jnp.float32).at[rows_idx].set(...]
  transfers between devices with their start and end apart: 26 -> 0, of which waited for: 25 -> 0; matrix products, arithmetic and copies ran while one was open for 3% -> 0% of each run, Pallas kernels for 0% -> 0%
where the time goes in v1:
time: 121 us
  Pallas kernels  103 us (85%)
  local copies, waits for them, and re-layouts  17.1 us (14%)
    pallas_call x1, Pallas kernels, body(): pl.pallas_call(functools.partial(kernel, dims), out_shape=(out, out), in_...  103 us
    unnamed x10, local copies, waits for them, and re-layouts  9.7 us
    pallas_call x2, local copies, waits for them, and re-layouts, body(): pl.pallas_call(functools.partial(kernel, dims), out_shape=(out, out), in_...  4.99 us

profile of v1, /device:TPU:1, one launch (start us, length us, event | category | flops | bytes accessed | tf_op | source)
XLA Modules:
  0.0 120.8 jit_solution(14705941420512416469)
XLA Ops:
  0.6 0.8 pad_slice_fusion.1
  1.4 0.7 reshape.11.idxr
  2.1 1.0 reshape.12.idxc
  3.0 0.0 copy-start.1
  3.0 2.1 %copy.17.corner = f32[1,1215,24]{2,1,0:T(8,128)} copy(f32[1,1215,24]{1,2,0:T(8,128)} %param.9) | data formatting | bytes 233280 | tf_op args[3]
  5.2 0.0 copy-start
  5.2 2.8 %copy.16.schur = f32[1,588,588]{2,1,0:T(8,128)} copy(f32[1,588,588]{2,0,1:T(1,128)} %param.8) | data formatting | bytes 2765952 | tf_op args[2]
  8.0 0.0 copy-done.1
  8.0 1.7 %copy.18.loads = f32[1,1215,512]{2,1,0:T(8,128)} copy(f32[1,1215,512]{2,0,1:T(1,128)S(1)} %copy-done.1) | data formatting | bytes 4976640 | tf_op args[5]
  9.7 0.0 copy-done
  9.7 3.0 %copy.15.kinv = f32[1,1215,1215]{2,1,0:T(8,128)} copy(f32[1,1215,1215]{2,0,1:T(1,128)S(1)} %copy-done) | data formatting | bytes 11809800 | tf_op args[1]
  12.7 103.1 %shard_map.77 = (f32[1,4,147,512]{3,2,1,0:T(8,128)}, f32[1,4,147,512]{3,2,1,0:T(8,128)}) custom-call(s32[640,1]{1,0:T(8,128)} %reshape.12.idxc, s32[1,640]{1,0:T(1,128)} %reshape.11.idxr, f32[1,1215,1215]{2,1,0:T(8,128)} %copy.15.kinv, f32[1,588,588]{2,1,0:T(8,128)} %copy.16.schur, f32[1,1215,24]{2,1,0:T(8,128)} %copy.17.corner, f32[186,744]{1,0:T(8,128)} %cinv.1, ...), custom_call_target="tpu_custom_call" | custom-call | tf_op jit(solution)/shard_map/pallas_call | solution.py:583
  115.8 0.0 copy-start.2
  115.8 3.2 %copy.19 = f32[1,4,147,512]{3,1,2,0:T(4,128)} copy(f32[1,4,147,512]{3,2,1,0:T(8,128)} %get-tuple-element.4) | data formatting | bytes 2408448 | tf_op jit(solution)/shard_map/pallas_call | solution.py:583
  119.0 0.0 copy-done.2
  119.0 1.8 %copy.20 = f32[1,4,147,512]{3,1,2,0:T(4,128)} copy(f32[1,4,147,512]{3,2,1,0:T(8,128)S(1)} %copy-done.2) | data formatting | bytes 2408448 | tf_op jit(solution)/shard_map/pallas_call | solution.py:583
  (1 shorter events, 0.0 us)
Async XLA Ops:
  3.0 4.9 %copy-start.1 = (f32[1,1215,512]{2,0,1:T(1,128)S(1)}, f32[1,1215,512]{2,0,1:T(1,128)}, u32[]{:S(2)}) copy-start(f32[1,1215,512]{2,0,1:T(1,128)} %param.11) | copy-start | bytes 7464964
  5.2 4.5 %copy-start = (f32[1,1215,1215]{2,0,1:T(1,128)S(1)}, f32[1,1215,1215]{2,0,1:T(1,128)}, u32[]{:S(2)}) copy-start(f32[1,1215,1215]{2,0,1:T(1,128)} %param.7) | copy-start | bytes 17714704
  115.8 3.2 %copy-start.2 = (f32[1,4,147,512]{3,2,1,0:T(8,128)S(1)}, f32[1,4,147,512]{3,2,1,0:T(8,128)}, u32[]{:S(2)}) copy-start(f32[1,4,147,512]{3,2,1,0:T(8,128)} %get-tuple-element.5) | copy-start | bytes 3612676

commit v2 on v1

v2 whole, which is shorter than its diff:
```python
import functools

import jax
import jax.numpy as jnp
from jax import lax
from jax.experimental import pallas as pl
from jax.experimental.pallas import tpu as pltpu
from jax.sharding import PartitionSpec as P

F32 = jnp.float32
BF16 = jnp.bfloat16
MESH = pl.DeviceIdType.MESH

FACE = 160
SENT = 152
NX = 4 * FACE
NC = 48
NW = 96
NA = NX + NC
ORDER = (2, 3, 0, 1)
LANES = 128


def dot(left, right):
    return jnp.dot(left, right, preferred_element_type=F32)


def dot_nt(left, right):
    return lax.dot_general(left, right, (((1,), (1,)), ((), ())), preferred_element_type=F32)


def split(value):
    high = value.astype(BF16)
    return high, (value - high.astype(F32)).astype(BF16)


def hot(cond, value=1.0):
    return jnp.where(cond, value, 0.0).astype(BF16)


def rows_of(shape):
    return lax.broadcasted_iota(jnp.int32, shape, 0)


def cols_of(shape):
    return lax.broadcasted_iota(jnp.int32, shape, 1)


def div(value, by):
    return (value * (65536 // by + 1)) >> 16


def kernel(dims, faces, kinv, schur, corner, cinv, loads, mo, ro,
           kv, lv, cv, sv, civ, khi, klo, tail, idxr, idxc, bmat, bmt, a0hi, a0lo, lhi, llo, a3, m3, w3, x3,
           cpad, cip, sp, tmat, tmt, ws, wo, wr, dall, dphi, dplo,
           tb, rb, rv, dv, mv, pbuf, p0, gb, sibs, sibr, hk, qk, hb, h3,
           rs, rr, er, co, outs,
           dsem, osem, fsend, frecv, wsend, wrecv, csend, crecv,
           s1s, s1r, s2s, s2r, bs, br, s3s, s3r, r1s, r1r, r2s, r2r):
    nsub, ncrs, nrows, fdof, cases, ncoarse = dims
    chips = nsub // 2
    nrp = khi.shape[1]
    cblock = ncoarse // ncrs
    cbp, ncp = cip.shape
    a = lax.axis_index("sub")
    b = lax.axis_index("crs")
    k = lax.div(a, 2)
    c = lax.rem(a, 2)
    sib = 2 * k + 1 - c
    up = lax.rem(a + 1, nsub)
    down = lax.rem(a + nsub - 1, nsub)
    left = lax.rem(b + ncrs - 1, ncrs)
    right = lax.rem(b + 1, ncrs)
    dests = ((a, left), (a, right), (down, b), (up, b))
    keeps = (None, None, a > 0, a < nsub - 1)
    drains = []

    def local(src, dst, n):
        return pltpu.make_async_copy(src, dst, dsem.at[n])

    def remote(src, dst, ssem, rsem, dev):
        return pltpu.make_async_remote_copy(
            src_ref=src, dst_ref=dst, send_sem=ssem, recv_sem=rsem, device_id=dev, device_id_type=MESH)

    def settle(ref, sem):
        pltpu.make_async_copy(ref, ref, sem).wait()

    in_copies = [local(corner.at[0], cv, 0), local(cinv, civ, 1), local(loads.at[:, 0], lv, 2),
                 local(kinv.at[:, 0], kv, 3), local(schur.at[:, 0], sv, 4)]
    for copy in in_copies:
        copy.start()

    barrier = pltpu.get_barrier_semaphore()
    for j in range(1, ncrs):
        pl.semaphore_signal(barrier, inc=1, device_id=(a, lax.rem(b + j, ncrs)), device_id_type=MESH)
    for j in range(ncrs):
        pl.semaphore_signal(barrier, inc=1, device_id=(up, j), device_id_type=MESH)
        pl.semaphore_signal(barrier, inc=1, device_id=(down, j), device_id_type=MESH)
    for j in range(1, ncrs):
        to = lax.rem(b + j, ncrs)
        pl.semaphore_signal(barrier, inc=1, device_id=(lax.rem(a + 2, nsub), to), device_id_type=MESH)
        pl.semaphore_signal(barrier, inc=1, device_id=(lax.rem(a + nsub - 2, nsub), to), device_id_type=MESH)

    def greet(j, carry):
        pl.semaphore_signal(barrier, inc=1, device_id=(2 * lax.rem(k + j, chips) + c, b), device_id_type=MESH)
        return carry

    lax.fori_loop(1, chips, greet, 0)

    greeted = ncrs - 1 + 2 * ncrs + 2 * (ncrs - 1) + chips - 1

    idxr[...] = jnp.full(idxr.shape, -1, jnp.int32)
    for pos in range(4):
        face = ORDER[pos]
        idxr[0:1, pos * FACE:pos * FACE + fdof] = faces[0, face:face + 1, :]
    idxc[...] = jnp.transpose(idxr[...])
    for pos in range(4):
        sign = 1.0 if pos % 2 else -1.0
        band = slice(pos * FACE, (pos + 1) * FACE)
        bmat[band, :] = hot(idxc[band, 0:1] == cols_of((FACE, nrp)), sign)
    lane = cols_of((1, NX))
    signs = jnp.where(((lane >= FACE) & (lane < 2 * FACE)) | (lane >= 3 * FACE), 1.0, -1.0)

    def build_bmt(i, carry):
        at = pl.multiple_of(i * LANES, LANES)
        rows = rows_of((LANES, NX)) + at
        bmt[pl.ds(at, LANES), :] = jnp.where(idxr[0:1, :] == rows, signs, 0.0).astype(BF16)
        return carry

    lax.fori_loop(0, nrp // LANES, build_bmt, 0)

    for n in range(2):
        for pos in range(4):
            rb[n, pos, SENT:FACE, :] = jnp.zeros((FACE - SENT, cases), F32)
    hb[:, 96:LANES, :] = jnp.zeros((3, 32, cases), F32)
    cpad[...] = jnp.zeros(cpad.shape, F32)
    cip[...] = jnp.zeros(cip.shape, F32)
    sp[...] = jnp.zeros(sp.shape, F32)
    edge = nrp - LANES
    khi[:, edge:] = jnp.zeros((nrp, LANES), BF16)
    klo[:, edge:] = jnp.zeros((nrp, LANES), BF16)
    whole = nrows // 16 * 16
    for ref in (khi, klo, lhi, llo):
        ref[whole:, :] = jnp.zeros((nrp - whole, ref.shape[1]), BF16)
    tail[...] = jnp.zeros(tail.shape, F32)

    in_copies[0].wait()
    ncl = cv.shape[0]
    cpad[0:ncl, 0:nrows] = cv[...]
    chi, clo = split(cpad[...])
    l = cols_of((1, 32))
    da = div(l, 12)
    rem12 = l - 12 * da
    db = div(rem12, 6)
    where_l = jnp.where(l < 24, 24 * da + 6 * lax.rem(b + db, ncrs) + rem12 - 6 * db, -1000)
    sel = hot(where_l == rows_of((NC, 32)))
    a0hi[0:NC, :] = dot(sel, chi).astype(BF16)
    a0lo[0:NC, :] = dot(sel, clo).astype(BF16)
    in_copies[2].wait()
    step = 16 * 5

    def split_loads(i, carry):
        at = pl.multiple_of(i * step, step)
        high, low = split(lv[pl.ds(at, step), :])
        lhi[pl.ds(at, step), :] = high
        llo[pl.ds(at, step), :] = low
        return carry

    lax.fori_loop(0, whole // step, split_loads, 0)
    left_rows = nrows - whole
    tail[0:left_rows, 0:cases] = lv[whole:nrows, :]
    high, low = split(tail[:, 0:cases])
    lhi[whole:whole + 16, :] = high
    llo[whole:whole + 16, :] = low

    def apply_loads(lo, hi):
        high, low = a0hi[lo:hi, :], a0lo[lo:hi, :]
        return dot(high, lhi[...]) + dot(high, llo[...]) + dot(low, lhi[...])

    def coarse_begin(f, offs):
        for i, off in enumerate(offs):
            owner = lax.rem(a + off + nsub, nsub)
            for j in range(ncrs):
                to = lax.rem(b + j, ncrs)
                at = pl.ds(pl.multiple_of(to * LANES, LANES), LANES)
                band = pl.ds(24 * i, 24)
                if off == 0 and j == 0:
                    p0[f, i * ncrs + b] = pbuf[f, band, at]
                    continue
                remote(pbuf.at[f, band, at], p0.at[f, i * ncrs + b], s1s.at[f], s1r.at[f], (owner, to)).start()
        drains.append(lambda: settle(p0.at[f, pl.ds(0, ncrs * len(offs) - 1)], s1s.at[f]))

    def coarse_gather(f, offs):
        count = ncrs * len(offs)
        settle(p0.at[f, pl.ds(0, count - 1)], s1r.at[f])
        gb[f, k] = jnp.sum(p0[f, 0:count], axis=0)

        def send(j, carry):
            to = 2 * lax.rem(k + j, chips) + c
            remote(gb.at[f, k], gb.at[f, k], s2s.at[f], s2r.at[f], (to, b)).start()
            return carry

        lax.fori_loop(1, chips, send, 0)
        drains.append(lambda: settle(gb.at[f, pl.ds(0, chips - 1)], s2s.at[f]))

    def coarse_solve(f):
        settle(gb.at[f, pl.ds(0, chips - 1)], s2r.at[f])
        high, low = split(gb[f].reshape(chips * 24, LANES))
        sibs[f, 0:LANES] = dot(dphi[...], high) + dot(dphi[...], low) + dot(dplo[...], high)
        sibs[f, LANES:LANES + 24] = gb[f, k]
        copy = remote(sibs.at[f], sibr.at[f], bs.at[f], br.at[f], (sib, b))
        copy.start()
        return copy

    def coarse_spread(f, copy, scale=None):
        copy.wait()
        at = pl.ds(pl.multiple_of(b * LANES, LANES), LANES)
        total = sibs[f, 0:LANES] + sibr[f, 0:LANES]
        mine, other = sibs[f, LANES:LANES + 24], sibr[f, LANES:LANES + 24]
        if scale is not None:
            part = scale[0:1, at]
            total = total + part * hk[...]
            mine = mine + part * qk[0]
            other = other + part * qk[1]
        hk[...] = total
        qk[0] = mine
        qk[1] = other
        hb[f, 0:96, at] = hk[pl.ds(pl.multiple_of(24 * c, 8), 96), :]
        for j in range(1, ncrs):
            remote(hb.at[f, pl.ds(0, 96), at], hb.at[f, pl.ds(0, 96), at], s3s.at[f], s3r.at[f],
                   (a, lax.rem(b + j, ncrs))).start()
        drains.append(lambda: settle(hb.at[f, pl.ds(0, 96), pl.ds(0, (ncrs - 1) * LANES)], s3s.at[f]))
        mine = hk[pl.ds(pl.multiple_of(24 + 24 * c, 8), 24), :] * mine
        other = hk[pl.ds(pl.multiple_of(48 - 24 * c, 8), 24), :] * other
        return 0.5 * jnp.sum(mine + other, axis=0, keepdims=True)

    def coarse_end(f):
        settle(hb.at[f, pl.ds(0, 96), pl.ds(0, (ncrs - 1) * LANES)], s3r.at[f])
        high, low = split(hb[f])
        h3[0:LANES, :] = high
        h3[LANES:2 * LANES, :] = low
        h3[2 * LANES:, :] = high

    row8 = rows_of((8, LANES))

    def packed(value):
        return jnp.concatenate([value[:, i * LANES:(i + 1) * LANES] for i in range(ncrs)], axis=0)

    def unpacked(value):
        return jnp.concatenate([value[i:i + 1] for i in range(ncrs)], axis=1)

    def sum_begin(n, first, second):
        rs[n] = jnp.concatenate([first, second], axis=0)
        for cc in range(2):
            for j in range(ncrs):
                if cc == 0 and j == 0:
                    rr[n, c * ncrs + b] = rs[n]
                    continue
                dev = (a if cc == 0 else sib, lax.rem(b + j, ncrs))
                remote(rs.at[n], rr.at[n, c * ncrs + b], r1s.at[n], r1r.at[n], dev).start()
        drains.append(lambda: settle(rr.at[n, pl.ds(0, 2 * ncrs - 1)], r1s.at[n]))

    def sum_gather(n):
        settle(rr.at[n, pl.ds(0, 2 * ncrs - 1)], r1r.at[n])
        er[n, k] = jnp.sum(rr[n], axis=0)

        def send(j, carry):
            to = 2 * lax.rem(k + j, chips) + c
            remote(er.at[n, k], er.at[n, k], r2s.at[n], r2r.at[n], (to, b)).start()
            return carry

        lax.fori_loop(1, chips, send, 0)
        drains.append(lambda: settle(er.at[n, pl.ds(0, chips - 1)], r2s.at[n]))

    def sum_end(n):
        settle(er.at[n, pl.ds(0, chips - 1)], r2r.at[n])
        total = jnp.sum(er[n], axis=0)
        return total[0:ncrs], total[ncrs:]

    def faces_start(n, which):
        copies = []
        for pos in which:
            copy = remote(tb.at[n % 2, pl.ds(pos * FACE, SENT)], rb.at[n % 2, pos ^ 1, pl.ds(0, SENT)],
                          fsend.at[n % 2, pos], frecv.at[n % 2, pos ^ 1], dests[pos])
            copy.start()
            copies.append(copy)
        return copies

    def faces_wait(copies):
        for copy in copies:
            copy.wait()

    def jumped(n, pos, extra=None):
        band = slice(pos * FACE, (pos + 1) * FACE)
        value = tb[n % 2, band, :] + rb[n % 2, pos]
        if extra is not None:
            value = value + extra
        if keeps[pos] is not None:
            value = jnp.where(keeps[pos], value, 0.0)
        return value

    def put_x(pos, value):
        high, low = split(value)
        lo = pos * FACE
        x3[lo:lo + FACE, :] = high
        x3[NX + lo:NX + lo + FACE, :] = low
        x3[2 * NX + lo:2 * NX + lo + FACE, :] = high

    pbuf[0, 0:NC] = apply_loads(0, NC)
    pl.semaphore_wait(barrier, greeted)
    coarse_begin(0, (0, 1))

    bch = dot_nt(bmat[...], chi).astype(BF16)
    bcl = dot_nt(bmat[...], clo).astype(BF16)
    l = rows_of((32, 1))
    da = div(l, 12)
    rem12 = l - 12 * da
    db = div(rem12, 6)
    where_l = 24 * (1 + da) + 6 * lax.rem(b + db, ncrs) + rem12 - 6 * db
    where_l = jnp.where(l < 24, where_l, -1000)
    lanes = cols_of((32, LANES))
    emaps = [hot(where_l + off == lanes) for off in (0, 24, -24)]
    wo[...] = dot(bch, emaps[0]) + dot(bcl, emaps[0])
    ws[0:2 * FACE, :] = wo[0:2 * FACE, :]
    for pos in (2, 3):
        band = slice(pos * FACE, (pos + 1) * FACE)
        ws[band, :] = dot(bch[band], emaps[pos - 1]) + dot(bcl[band], emaps[pos - 1])
    wcopies = [remote(ws.at[pl.ds(pos * FACE, FACE)], wr.at[pl.ds((pos ^ 1) * FACE, FACE)],
                      wsend.at[pos], wrecv.at[pos ^ 1], dests[pos]) for pos in range(4)]
    for copy in wcopies:
        copy.start()

    in_copies[1].wait()
    cip[0:cblock, 0:ncoarse] = civ[...]
    high, low = split(cip[...])
    i = cols_of((1, cbp))
    r = cblock * b + i
    plane = div(r, 24)
    base = lax.div(lax.div(cblock * b, 24), 2)
    target = 24 * ((plane >> 1) - base) + r - 24 * plane
    target = jnp.where((((plane + 1) & 1) == c) & (i < cblock), target, -1)
    pct = hot(target == rows_of((LANES, cbp)))
    x1h = dot(pct, high).astype(BF16)
    x1l = dot(pct, low).astype(BF16)
    i = rows_of((LANES, 1))
    r = 48 * k - 48 + i
    r = jnp.where((i < 120) & (r < ncoarse), r, -1)
    sel = hot(r == cols_of((LANES, ncp)))
    dall[b] = dot_nt(sel, x1h) + dot_nt(sel, x1l)
    for j in range(1, ncrs):
        remote(dall.at[b], dall.at[b], csend.at[j], crecv.at[j], (a, lax.rem(b + j, ncrs))).start()

    in_copies[3].wait()

    def split_k(i, carry):
        at = pl.multiple_of(i * step, step)
        high, low = split(kv[pl.ds(at, step), :])
        khi[pl.ds(at, step), 0:nrows] = high
        klo[pl.ds(at, step), 0:nrows] = low
        return carry

    lax.fori_loop(0, whole // step, split_k, 0)
    tail[0:left_rows, 0:nrows] = kv[whole:nrows, :]
    high, low = split(tail[...])
    khi[whole:whole + 16, :] = high
    klo[whole:whole + 16, :] = low

    def face_rows(lo, hi):
        def tile(i, carry):
            at = pl.ds(pl.multiple_of(i * 256, 256), 256)
            a0hi[NC + lo:NC + hi, at] = dot(bmat[lo:hi, :], khi[:, at]).astype(BF16)
            a0lo[NC + lo:NC + hi, at] = dot(bmat[lo:hi, :], klo[:, at]).astype(BF16)
            return carry

        lax.fori_loop(0, nrp // 256, tile, 0)

    half = 2 * FACE
    face_rows(0, half)
    tb[0, 0:half, :] = apply_loads(NC, NC + half)
    copies = faces_start(0, (0, 1))
    coarse_gather(0, (0, 1))
    face_rows(half, NX)
    tb[0, half:NX, :] = apply_loads(NC + half, NC + NX)
    copies += faces_start(0, (2, 3))

    for j in range(1, ncrs):
        copy = remote(dall.at[b], dall.at[b], csend.at[j], crecv.at[j], (a, lax.rem(b + j, ncrs)))
        copy.wait()
    total_hi = total_lo = None
    for blk_b in range(ncrs):
        j = rows_of((LANES, 1))
        pair = div(j, 24)
        rem = j - 24 * pair
        pair = pair + (cblock * blk_b // 24) // 2
        r = 24 * (2 * pair + 1 - c) + rem
        target = jnp.where((j < 120) & (r >= cblock * blk_b) & (r < cblock * (blk_b + 1)),
                           24 * (pair + 1 - c) + rem, -1)
        perm = hot(target == cols_of((LANES, chips * 24)))
        high, low = split(dall[blk_b])
        ph, plo = dot(high, perm), dot(low, perm)
        total_hi = ph if total_hi is None else total_hi + ph
        total_lo = plo if total_lo is None else total_lo + plo
    dphi[...] = total_hi.astype(BF16)
    dplo[...] = total_lo.astype(BF16)

    coarse_copy = coarse_solve(0)

    def between(i, carry):
        at = pl.ds(pl.multiple_of(i * half, half), half)
        src = pl.ds(pl.multiple_of(NC + i * half, 16), half)
        high = dot(a0hi[src, :], bmt[...]).astype(BF16)
        a3[at, 0:NX] = high
        a3[at, NX:2 * NX] = high
        a3[at, 2 * NX:] = dot(a0lo[src, :], bmt[...]).astype(BF16)
        return carry

    lax.fori_loop(0, 2, between, 0)
    coarse_spread(0, coarse_copy)

    in_copies[4].wait()
    nface = sv.shape[0]
    sp[0:nface, 0:nface] = sv[...]
    high, low = split(sp[...])
    khi[0:NX, 0:NX] = high
    klo[0:NX, 0:NX] = low
    for pos in range(4):
        face = ORDER[pos]
        sign = 0.5 if pos % 2 else -0.5
        j = rows_of((FACE, 1))
        target = jnp.where(j < fdof, j + face * fdof, -1)
        tmat[pos * FACE:(pos + 1) * FACE, :] = hot(target == cols_of((FACE, NX)), sign)
    pos_l = jnp.where(lane >= FACE, 1, 0) + jnp.where(lane >= 2 * FACE, 1, 0) + jnp.where(lane >= 3 * FACE, 1, 0)
    j = lane - FACE * pos_l
    target = jnp.where(j < fdof, j + fdof * ((pos_l + 2) & 3), -1)
    kept = jnp.where(pos_l == 2, jnp.where(a > 0, 0.5, 0.0), jnp.where(pos_l == 3, jnp.where(a < nsub - 1, 0.5, 0.0), 0.5))
    tmt[...] = jnp.where(target == rows_of((NX, NX)), signs * kept, 0.0).astype(BF16)

    def precond_rows(i, carry):
        at = pl.ds(pl.multiple_of(i * FACE, FACE), FACE)
        high = dot(tmat[at, :], khi[0:NX, 0:NX]).astype(BF16)
        low = dot(tmat[at, :], klo[0:NX, 0:NX]).astype(BF16)
        high = dot(high, tmt[...]).astype(BF16)
        to = pl.ds(pl.multiple_of(NW + i * FACE, 16), FACE)
        m3[to, 0:NX] = high
        m3[to, NX:2 * NX] = high
        m3[to, 2 * NX:] = dot(low, tmt[...]).astype(BF16)
        return carry

    lax.fori_loop(0, 4, precond_rows, 0)

    for copy in wcopies:
        copy.wait()
    for pos in range(4):
        band = slice(pos * FACE, (pos + 1) * FACE)
        value = wo[band, :] + wr[band, :]
        if keeps[pos] is not None:
            value = jnp.where(keeps[pos], value, 0.0)
        wo[band, :] = value
    high, low = split(wo[...])
    w3[:, 0:LANES] = high
    w3[:, LANES:2 * LANES] = high
    w3[:, 2 * LANES:] = low
    high, low = split(jnp.transpose(wo[...]))
    mhi, mlo = m3[NW:, 0:NX], m3[NW:, 2 * NX:]
    high, low = split((dot(high, mhi) + dot(high, mlo) + dot(low, mhi))[0:NW])
    m3[0:NW, 0:NX] = high
    m3[0:NW, NX:2 * NX] = high
    m3[0:NW, 2 * NX:] = low

    def operator_end(n, f, copies, use):
        coarse_end(f)
        faces_wait(copies)
        for pos in range(4):
            use(pos, jumped(n, pos, dot(w3[pos * FACE:(pos + 1) * FACE, :], h3[...])))

    def first_use(pos, value):
        rv[pos * FACE:(pos + 1) * FACE, :] = value
        put_x(pos, value)

    operator_end(0, 0, copies, first_use)

    around = (-1, 0, 1, 2)

    def precond(n, f):
        block = dot(m3[0:NW + half, :], x3[...])
        pbuf[f] = block[0:NW]
        coarse_begin(f, around)
        tb[n % 2, 0:half, :] = block[NW:]
        copies = faces_start(n, (0, 1))
        tb[n % 2, half:, :] = dot(m3[NW + half:, :], x3[...])
        copies += faces_start(n, (2, 3))
        return copies, packed(jnp.sum(rv[...] * tb[n % 2], axis=0, keepdims=True))

    def operator(n, f, rz_part, scale):
        tb[n % 2, 0:half, :] = dot(a3[0:half, :], x3[...])
        copies = faces_start(n, (0, 1))
        coarse_copy = coarse_solve(f)
        tb[n % 2, half:, :] = dot(a3[half:, :], x3[...])
        copies += faces_start(n, (2, 3))
        energy = packed(jnp.sum(dv[...] * tb[n % 2], axis=0, keepdims=True))
        ce = coarse_spread(f, coarse_copy, scale)
        energy = energy + jnp.where(rows_of((ncrs, LANES)) == b, ce, 0.0)
        sum_begin(f, rz_part, energy)
        sum_gather(f)
        return copies

    def keep_image(n):
        def use(pos, value):
            tb[n % 2, pos * FACE:(pos + 1) * FACE, :] = value
        return use

    copies, rz_part = precond(1, 1)
    coarse_gather(1, around)
    faces_wait(copies)
    for pos in range(4):
        value = jumped(1, pos)
        dv[pos * FACE:(pos + 1) * FACE, :] = value
        put_x(pos, value)

    copies = operator(2, 1, rz_part, None)
    operator_end(2, 1, copies, keep_image(2))
    rz_now, energy = sum_end(1)
    alpha = unpacked(rz_now / energy)
    for pos in range(4):
        band = slice(pos * FACE, (pos + 1) * FACE)
        value = rv[band, :] - alpha * tb[0, band, :]
        rv[band, :] = value
        put_x(pos, value)

    copies, rz_part = precond(3, 2)
    sum_begin(0, rz_part, jnp.zeros((ncrs, LANES), F32))
    coarse_gather(2, around)
    sum_gather(0)
    for pos in range(4):
        band = slice(pos * FACE, (pos + 1) * FACE)
        mv[band, :] = alpha * dv[band, :]
    faces_wait(copies)
    rz_next, _ = sum_end(0)
    beta = unpacked(rz_next / rz_now)
    co[0:1, :] = beta
    for pos in range(4):
        band = slice(pos * FACE, (pos + 1) * FACE)
        value = jumped(3, pos) + beta * dv[band, :]
        dv[band, :] = value
        put_x(pos, value)

    copies = operator(4, 2, rz_next, co)
    operator_end(4, 2, copies, keep_image(4))
    _, energy = sum_end(2)
    alpha = unpacked(rz_next / energy)
    out_copies = []
    for pos in range(4):
        band = slice(pos * FACE, (pos + 1) * FACE)
        outs[pos] = (mv[band, :] + alpha * dv[band, :])[0:fdof]
        outs[4 + pos] = (rv[band, :] - alpha * tb[0, band, :])[0:fdof]
        for side, ref in enumerate((mo, ro)):
            copy = pltpu.make_async_copy(outs.at[4 * side + pos], ref.at[0, :, ORDER[pos]], osem.at[4 * side + pos])
            copy.start()
            out_copies.append(copy)
    for copy in out_copies:
        copy.wait()

    for drain in drains:
        drain()


def body(face_index, kinv, schur, corner, coarse_inverse, loads):
    nsub = lax.axis_size("sub")
    ncrs = lax.axis_size("crs")
    fdof = face_index.shape[2]
    nrows, cases = loads.shape[1:]
    ncoarse = coarse_inverse.shape[1]
    nface = schur.shape[1]
    ncl = corner.shape[2]
    chips = nsub // 2
    nrp = -(-nrows // 256) * 256
    cbp = -(-coarse_inverse.shape[0] // 16) * 16
    ncp = -(-ncoarse // LANES) * LANES
    vm = pltpu.VMEM
    dma = pltpu.SemaphoreType.DMA
    scratch = [
        vm((nrows, nrows), F32), vm((nrows, cases), F32), vm((ncl, nrows), F32), vm((nface, nface), F32),
        vm(coarse_inverse.shape, F32),
        vm((nrp, nrp), BF16), vm((nrp, nrp), BF16), vm((16, nrp), F32),
        vm((8, NX), jnp.int32), vm((NX, 8), jnp.int32),
        vm((NX, nrp), BF16), vm((nrp, NX), BF16), vm((NA, nrp), BF16), vm((NA, nrp), BF16),
        vm((nrp, cases), BF16), vm((nrp, cases), BF16),
        vm((NX, 3 * NX), BF16), vm((NW + NX, 3 * NX), BF16), vm((NX, 3 * LANES), BF16), vm((3 * NX, cases), BF16),
        vm((32, nrp), F32), vm((cbp, ncp), F32),
        vm((NX, NX), F32), vm((NX, NX), BF16), vm((NX, NX), BF16),
        vm((NX, LANES), F32), vm((NX, LANES), F32), vm((NX, LANES), F32),
        vm((ncrs, LANES, LANES), F32), vm((LANES, chips * 24), BF16), vm((LANES, chips * 24), BF16),
        vm((2, NX, cases), F32), vm((2, 4, FACE, cases), F32),
        vm((NX, cases), F32), vm((NX, cases), F32), vm((NX, cases), F32),
        vm((3, NW, cases), F32), vm((3, 4 * ncrs, 24, LANES), F32), vm((3, chips, 24, LANES), F32),
        vm((3, LANES + 24, LANES), F32), vm((3, LANES + 24, LANES), F32), vm((LANES, LANES), F32),
        vm((2, 24, LANES), F32), vm((3, LANES, cases), F32), vm((3 * LANES, cases), BF16),
        vm((3, 8, LANES), F32), vm((3, 2 * ncrs, 8, LANES), F32), vm((3, chips, 8, LANES), F32),
        vm((8, cases), F32), vm((8, fdof, cases), F32),
        dma((5,)), dma((8,)), dma((2, 4)), dma((2, 4)), dma((4,)), dma((4,)), dma((ncrs,)), dma((ncrs,)),
    ] + [dma((3,)) for _ in range(12)]
    out = jax.ShapeDtypeStruct((1, fdof, 4, cases), F32)
    anyspace = pl.BlockSpec(memory_space=pl.ANY)
    inside = pl.BlockSpec(memory_space=pltpu.VMEM)
    dims = (nsub, ncrs, nrows, fdof, cases, ncoarse)
    mult, resid = pl.pallas_call(
        functools.partial(kernel, dims),
        out_shape=(out, out),
        in_specs=[inside] + [anyspace] * 5,
        out_specs=(anyspace, anyspace),
        scratch_shapes=scratch,
        compiler_params=pltpu.CompilerParams(
            collective_id=0, has_side_effects=True, vmem_limit_bytes=63 * 2**20),
    )(face_index, jnp.swapaxes(kinv, 0, 1), jnp.swapaxes(schur, 0, 1),
      jnp.swapaxes(corner, 1, 2), coarse_inverse, jnp.swapaxes(loads, 0, 1))
    return jnp.swapaxes(mult, 1, 2), jnp.swapaxes(resid, 1, 2)


def solution(mesh):
    subs = P(("sub", "crs"), None, None)
    out = P(("sub", "crs"), None, None, None)
    return jax.shard_map(
        body, mesh=mesh, in_specs=(subs, subs, subs, subs, P("crs", None), subs), out_specs=(out, out),
        check_vma=False)
```

time: 121 us -> 99.5 us (0.82)
  local copies, waits for them, and re-layouts: 17.1 us -> 3.63 us
  Pallas kernels: 103 us -> 95 us
    pallas_call x1, Pallas kernels: 103 us -> 95 us  [body(): pl.pallas_call(functools.partial(kernel, dims), out_shape=(out, out), in_...]
    unnamed x10 -> x4, local copies, waits for them, and re-layouts: 9.7 us -> 3.63 us
    pallas_call x2 -> x0, local copies, waits for them, and re-layouts: 4.99 us -> none  [body(): pl.pallas_call(functools.partial(kernel, dims), out_shape=(out, out), in_...]
    reshape x2 -> x0, local copies, waits for them, and re-layouts: 1.63 us -> none  [the longest x1 0.97 us: body(): idx.reshape(NX, 1)]
where the time goes in v2:
time: 99.5 us; the launch traced here: 99.3 us
  Pallas kernels  95 us (95%)
  local copies, waits for them, and re-layouts  3.63 us (4%)
    pallas_call x1, Pallas kernels, body(): pl.pallas_call(functools.partial(kernel, dims), out_shape=(out, out), in_...  95 us
    unnamed x4, local copies, waits for them, and re-layouts  3.63 us

profile of v2, /device:TPU:1, one launch (start us, length us, event | category | flops | bytes accessed | tf_op | source)
XLA Modules:
  0.0 99.3 jit_solution(9227820132405805380)
XLA Ops:
  0.6 95.0 %shard_map.77 = (f32[1,147,4,512]{3,2,1,0:T(4,128)}, f32[1,147,4,512]{3,2,1,0:T(4,128)}) custom-call(s32[1,4,147]{2,1,0:T(4,128)} %faces.1, f32[1215,1,1215]{2,1,0:T(1,128)} %bitcast.6, f32[588,1,588]{2,1,0:T(1,128)} %bitcast.8, f32[1,24,1215]{2,1,0:T(8,128)} %bitcast.11, f32[186,744]{1,0:T(8,128)} %cinv.1, f32[1215,1,512]{2,1,0:T(1,128)} %bitcast.7), custom_call_target="tpu_custom_call" | custom-call | tf_op jit(solution)/shard_map/pallas_call | solution.py:606
  95.7 0.0 copy-start
  95.7 2.6 %copy.10 = f32[1,4,147,512]{3,1,2,0:T(4,128)} copy(f32[1,4,147,512]{3,1,2,0:T(4,128)} %bitcast.10) | data formatting | bytes 2408448
  98.3 0.0 copy-done
  98.3 1.0 %copy.11 = f32[1,4,147,512]{3,1,2,0:T(4,128)} copy(f32[1,4,147,512]{3,1,2,0:T(4,128)S(1)} %bitcast.9) | data formatting | bytes 2408448
Async XLA Ops:
  95.7 2.6 %copy-start = (f32[1,147,4,512]{3,2,1,0:T(4,128)S(1)}, f32[1,147,4,512]{3,2,1,0:T(4,128)}, u32[]{:S(2)}) copy-start(f32[1,147,4,512]{3,2,1,0:T(4,128)} %get-tuple-element.5) | copy-start | bytes 3612676

commit v3 on v2

--- a/solution.py
+++ b/solution.py
@@ -53,7 +53,7 @@
 def kernel(dims, faces, kinv, schur, corner, cinv, loads, mo, ro,
            kv, lv, cv, sv, civ, khi, klo, tail, idxr, idxc, bmat, bmt, a0hi, a0lo, lhi, llo, a3, m3, w3, x3,
            cpad, cip, sp, tmat, tmt, ws, wo, wr, dall, dphi, dplo,
-           tb, rb, rv, dv, mv, pbuf, p0, gb, sibs, sibr, hk, qk, hb, h3,
+           tb, rb, rv, dv, mv, pbuf, p0, gb, sibs, sibr, hs, hk, qk, hb, h3,
            rs, rr, er, co, outs,
            dsem, osem, fsend, frecv, wsend, wrecv, csend, crecv,
            s1s, s1r, s2s, s2r, bs, br, s3s, s3r, r1s, r1r, r2s, r2r):
@@ -212,11 +212,20 @@
         copy.start()
         return copy
 
-    def coarse_spread(f, copy, scale=None):
+    def coarse_spread(f, copy):
         copy.wait()
         at = pl.ds(pl.multiple_of(b * LANES, LANES), LANES)
         total = sibs[f, 0:LANES] + sibr[f, 0:LANES]
-        mine, other = sibs[f, LANES:LANES + 24], sibr[f, LANES:LANES + 24]
+        hs[...] = total
+        hb[f, 0:NW, at] = hs[pl.ds(pl.multiple_of(24 * c, 8), NW), :]
+        for j in range(1, ncrs):
+            remote(hb.at[f, pl.ds(0, NW), at], hb.at[f, pl.ds(0, NW), at], s3s.at[f], s3r.at[f],
+                   (a, lax.rem(b + j, ncrs))).start()
+        drains.append(lambda: settle(hb.at[f, pl.ds(0, NW), pl.ds(0, (ncrs - 1) * LANES)], s3s.at[f]))
+
+    def coarse_energy(f, scale=None):
+        at = pl.ds(pl.multiple_of(b * LANES, LANES), LANES)
+        total, mine, other = hs[...], sibs[f, LANES:LANES + 24], sibr[f, LANES:LANES + 24]
         if scale is not None:
             part = scale[0:1, at]
             total = total + part * hk[...]
@@ -225,18 +234,16 @@
         hk[...] = total
         qk[0] = mine
         qk[1] = other
-        hb[f, 0:96, at] = hk[pl.ds(pl.multiple_of(24 * c, 8), 96), :]
-        for j in range(1, ncrs):
-            remote(hb.at[f, pl.ds(0, 96), at], hb.at[f, pl.ds(0, 96), at], s3s.at[f], s3r.at[f],
-                   (a, lax.rem(b + j, ncrs))).start()
-        drains.append(lambda: settle(hb.at[f, pl.ds(0, 96), pl.ds(0, (ncrs - 1) * LANES)], s3s.at[f]))
         mine = hk[pl.ds(pl.multiple_of(24 + 24 * c, 8), 24), :] * mine
         other = hk[pl.ds(pl.multiple_of(48 - 24 * c, 8), 24), :] * other
         return 0.5 * jnp.sum(mine + other, axis=0, keepdims=True)
 
-    def coarse_end(f):
+    def coarse_end(f, scale=None):
         settle(hb.at[f, pl.ds(0, 96), pl.ds(0, (ncrs - 1) * LANES)], s3r.at[f])
-        high, low = split(hb[f])
+        value = hb[f]
+        if scale is not None:
+            value = value + scale[0:1, :] * hb[f - 1]
+        high, low = split(value)
         h3[0:LANES, :] = high
         h3[LANES:2 * LANES, :] = low
         h3[2 * LANES:, :] = high
@@ -307,9 +314,6 @@
         x3[2 * NX + lo:2 * NX + lo + FACE, :] = high
 
     pbuf[0, 0:NC] = apply_loads(0, NC)
-    pl.semaphore_wait(barrier, greeted)
-    coarse_begin(0, (0, 1))
-
     bch = dot_nt(bmat[...], chi).astype(BF16)
     bcl = dot_nt(bmat[...], clo).astype(BF16)
     l = rows_of((32, 1))
@@ -327,8 +331,6 @@
         ws[band, :] = dot(bch[band], emaps[pos - 1]) + dot(bcl[band], emaps[pos - 1])
     wcopies = [remote(ws.at[pl.ds(pos * FACE, FACE)], wr.at[pl.ds((pos ^ 1) * FACE, FACE)],
                       wsend.at[pos], wrecv.at[pos ^ 1], dests[pos]) for pos in range(4)]
-    for copy in wcopies:
-        copy.start()
 
     in_copies[1].wait()
     cip[0:cblock, 0:ncoarse] = civ[...]
@@ -347,9 +349,6 @@
     r = jnp.where((i < 120) & (r < ncoarse), r, -1)
     sel = hot(r == cols_of((LANES, ncp)))
     dall[b] = dot_nt(sel, x1h) + dot_nt(sel, x1l)
-    for j in range(1, ncrs):
-        remote(dall.at[b], dall.at[b], csend.at[j], crecv.at[j], (a, lax.rem(b + j, ncrs))).start()
-
     in_copies[3].wait()
 
     def split_k(i, carry):
@@ -376,10 +375,16 @@
 
     half = 2 * FACE
     face_rows(0, half)
+    pl.semaphore_wait(barrier, greeted)
+    coarse_begin(0, (0, 1))
+    for copy in wcopies:
+        copy.start()
+    for j in range(1, ncrs):
+        remote(dall.at[b], dall.at[b], csend.at[j], crecv.at[j], (a, lax.rem(b + j, ncrs))).start()
     tb[0, 0:half, :] = apply_loads(NC, NC + half)
     copies = faces_start(0, (0, 1))
+    face_rows(half, NX)
     coarse_gather(0, (0, 1))
-    face_rows(half, NX)
     tb[0, half:NX, :] = apply_loads(NC + half, NC + NX)
     copies += faces_start(0, (2, 3))
 
@@ -403,8 +408,6 @@
     dphi[...] = total_hi.astype(BF16)
     dplo[...] = total_lo.astype(BF16)
 
-    coarse_copy = coarse_solve(0)
-
     def between(i, carry):
         at = pl.ds(pl.multiple_of(i * half, half), half)
         src = pl.ds(pl.multiple_of(NC + i * half, 16), half)
@@ -415,7 +418,7 @@
         return carry
 
     lax.fori_loop(0, 2, between, 0)
-    coarse_spread(0, coarse_copy)
+    coarse_copy = coarse_solve(0)
 
     in_copies[4].wait()
     nface = sv.shape[0]
@@ -446,6 +449,7 @@
         m3[to, 2 * NX:] = dot(low, tmt[...]).astype(BF16)
         return carry
 
+    coarse_spread(0, coarse_copy)
     lax.fori_loop(0, 4, precond_rows, 0)
 
     for copy in wcopies:
@@ -467,8 +471,8 @@
     m3[0:NW, NX:2 * NX] = high
     m3[0:NW, 2 * NX:] = low
 
-    def operator_end(n, f, copies, use):
-        coarse_end(f)
+    def operator_end(n, f, copies, use, scale=None):
+        coarse_end(f, scale)
         faces_wait(copies)
         for pos in range(4):
             use(pos, jumped(n, pos, dot(w3[pos * FACE:(pos + 1) * FACE, :], h3[...])))
@@ -481,26 +485,35 @@
 
     around = (-1, 0, 1, 2)
 
-    def precond(n, f):
+    def precond(n, f, total):
         block = dot(m3[0:NW + half, :], x3[...])
         pbuf[f] = block[0:NW]
         coarse_begin(f, around)
         tb[n % 2, 0:half, :] = block[NW:]
-        copies = faces_start(n, (0, 1))
+        copies = []
+        if total is None:
+            copies += faces_start(n, (0, 1))
         tb[n % 2, half:, :] = dot(m3[NW + half:, :], x3[...])
-        copies += faces_start(n, (2, 3))
-        return copies, packed(jnp.sum(rv[...] * tb[n % 2], axis=0, keepdims=True))
+        if total is None:
+            copies += faces_start(n, (2, 3))
+        rz_part = packed(jnp.sum(rv[...] * tb[n % 2], axis=0, keepdims=True))
+        if total is not None:
+            sum_begin(total, rz_part, jnp.zeros((ncrs, LANES), F32))
+            copies += faces_start(n, (0, 1, 2, 3))
+        coarse_gather(f, around)
+        if total is not None:
+            sum_gather(total)
+        coarse_copy = coarse_solve(f)
+        faces_wait(copies)
+        return coarse_copy, rz_part
 
     def operator(n, f, rz_part, scale):
         tb[n % 2, 0:half, :] = dot(a3[0:half, :], x3[...])
-        copies = faces_start(n, (0, 1))
-        coarse_copy = coarse_solve(f)
         tb[n % 2, half:, :] = dot(a3[half:, :], x3[...])
-        copies += faces_start(n, (2, 3))
         energy = packed(jnp.sum(dv[...] * tb[n % 2], axis=0, keepdims=True))
-        ce = coarse_spread(f, coarse_copy, scale)
-        energy = energy + jnp.where(rows_of((ncrs, LANES)) == b, ce, 0.0)
+        energy = energy + jnp.where(rows_of((ncrs, LANES)) == b, coarse_energy(f, scale), 0.0)
         sum_begin(f, rz_part, energy)
+        copies = faces_start(n, (0, 1, 2, 3))
         sum_gather(f)
         return copies
 
@@ -509,14 +522,13 @@
             tb[n % 2, pos * FACE:(pos + 1) * FACE, :] = value
         return use
 
-    copies, rz_part = precond(1, 1)
-    coarse_gather(1, around)
-    faces_wait(copies)
+    coarse_copy, rz_part = precond(1, 1, None)
     for pos in range(4):
         value = jumped(1, pos)
         dv[pos * FACE:(pos + 1) * FACE, :] = value
         put_x(pos, value)
 
+    coarse_spread(1, coarse_copy)
     copies = operator(2, 1, rz_part, None)
     operator_end(2, 1, copies, keep_image(2))
     rz_now, energy = sum_end(1)
@@ -527,14 +539,11 @@
         rv[band, :] = value
         put_x(pos, value)
 
-    copies, rz_part = precond(3, 2)
-    sum_begin(0, rz_part, jnp.zeros((ncrs, LANES), F32))
-    coarse_gather(2, around)
-    sum_gather(0)
+    coarse_copy, rz_part = precond(3, 2, 0)
+    coarse_spread(2, coarse_copy)
     for pos in range(4):
         band = slice(pos * FACE, (pos + 1) * FACE)
         mv[band, :] = alpha * dv[band, :]
-    faces_wait(copies)
     rz_next, _ = sum_end(0)
     beta = unpacked(rz_next / rz_now)
     co[0:1, :] = beta
@@ -545,7 +554,7 @@
         put_x(pos, value)
 
     copies = operator(4, 2, rz_next, co)
-    operator_end(4, 2, copies, keep_image(4))
+    operator_end(4, 2, copies, keep_image(4), co)
     _, energy = sum_end(2)
     alpha = unpacked(rz_next / energy)
     out_copies = []
@@ -593,7 +602,7 @@
         vm((2, NX, cases), F32), vm((2, 4, FACE, cases), F32),
         vm((NX, cases), F32), vm((NX, cases), F32), vm((NX, cases), F32),
         vm((3, NW, cases), F32), vm((3, 4 * ncrs, 24, LANES), F32), vm((3, chips, 24, LANES), F32),
-        vm((3, LANES + 24, LANES), F32), vm((3, LANES + 24, LANES), F32), vm((LANES, LANES), F32),
+        vm((3, LANES + 24, LANES), F32), vm((3, LANES + 24, LANES), F32), vm((LANES, LANES), F32), vm((LANES, LANES), F32),
         vm((2, 24, LANES), F32), vm((3, LANES, cases), F32), vm((3 * LANES, cases), BF16),
         vm((3, 8, LANES), F32), vm((3, 2 * ncrs, 8, LANES), F32), vm((3, chips, 8, LANES), F32),
         vm((8, cases), F32), vm((8, fdof, cases), F32),

time: 99.5 us -> 94.2 us (0.947)
  Pallas kernels: 95 us -> 89.7 us
    pallas_call x1, Pallas kernels: 95 us -> 89.7 us  [body(): pl.pallas_call(functools.partial(kernel, dims), out_shape=(out, out), in_...]
where the time goes in v3:
time: 94.2 us; the launch traced here: 94 us
  Pallas kernels  89.7 us (95%)
  local copies, waits for them, and re-layouts  3.63 us (4%)
    pallas_call x1, Pallas kernels, body(): pl.pallas_call(functools.partial(kernel, dims), out_shape=(out, out), in_...  89.7 us
    unnamed x4, local copies, waits for them, and re-layouts  3.63 us

profile of v3, /device:TPU:1, one launch (start us, length us, event | category | flops | bytes accessed | tf_op | source)
XLA Modules:
  0.0 94.0 jit_solution(7044834433374479927)
XLA Ops:
  0.6 89.7 %shard_map.77 = (f32[1,147,4,512]{3,2,1,0:T(4,128)}, f32[1,147,4,512]{3,2,1,0:T(4,128)}) custom-call(s32[1,4,147]{2,1,0:T(4,128)} %faces.1, f32[1215,1,1215]{2,1,0:T(1,128)} %bitcast.6, f32[588,1,588]{2,1,0:T(1,128)} %bitcast.8, f32[1,24,1215]{2,1,0:T(8,128)} %bitcast.11, f32[186,744]{1,0:T(8,128)} %cinv.1, f32[1215,1,512]{2,1,0:T(1,128)} %bitcast.7), custom_call_target="tpu_custom_call" | custom-call | tf_op jit(solution)/shard_map/pallas_call | solution.py:615
  90.4 0.0 copy-start
  90.4 2.6 %copy.10 = f32[1,4,147,512]{3,1,2,0:T(4,128)} copy(f32[1,4,147,512]{3,1,2,0:T(4,128)} %bitcast.10) | data formatting | bytes 2408448
  93.0 0.0 copy-done
  93.0 1.0 %copy.11 = f32[1,4,147,512]{3,1,2,0:T(4,128)} copy(f32[1,4,147,512]{3,1,2,0:T(4,128)S(1)} %bitcast.9) | data formatting | bytes 2408448
Async XLA Ops:
  90.4 2.6 %copy-start = (f32[1,147,4,512]{3,2,1,0:T(4,128)S(1)}, f32[1,147,4,512]{3,2,1,0:T(4,128)}, u32[]{:S(2)}) copy-start(f32[1,147,4,512]{3,2,1,0:T(4,128)} %get-tuple-element.5) | copy-start | bytes 3612676

commit v4 on v3

--- a/solution.py
+++ b/solution.py
@@ -52,7 +52,7 @@
 
 def kernel(dims, faces, kinv, schur, corner, cinv, loads, mo, ro,
            kv, lv, cv, sv, civ, khi, klo, tail, idxr, idxc, bmat, bmt, a0hi, a0lo, lhi, llo, a3, m3, w3, x3,
-           cpad, cip, sp, tmat, tmt, ws, wo, wr, dall, dphi, dplo,
+           cpad, cip, sp, tmt, ws, wo, wr, dall, dphi, dplo,
            tb, rb, rv, dv, mv, pbuf, p0, gb, sibs, sibr, hs, hk, qk, hb, h3,
            rs, rr, er, co, outs,
            dsem, osem, fsend, frecv, wsend, wrecv, csend, crecv,
@@ -86,7 +86,8 @@
         pltpu.make_async_copy(ref, ref, sem).wait()
 
     in_copies = [local(corner.at[0], cv, 0), local(cinv, civ, 1), local(loads.at[:, 0], lv, 2),
-                 local(kinv.at[:, 0], kv, 3), local(schur.at[:, 0], sv, 4)]
+                 local(kinv.at[:, 0], kv, 3)]
+    in_copies += [local(schur.at[pl.ds(ORDER[pos] * fdof, fdof), 0], sv.at[pos], 4 + pos) for pos in range(4)]
     for copy in in_copies:
         copy.start()
 
@@ -284,6 +285,34 @@
         total = jnp.sum(er[n], axis=0)
         return total[0:ncrs], total[ncrs:]
 
+    def late_begin(n, first, second):
+        er[n, k] = jnp.concatenate([first, second], axis=0)
+
+        def send(j, carry):
+            to = 2 * lax.rem(k + j, chips) + c
+            remote(er.at[n, k], er.at[n, k], r2s.at[n], r2r.at[n], (to, b)).start()
+            return carry
+
+        lax.fori_loop(1, chips, send, 0)
+        drains.append(lambda: settle(er.at[n, pl.ds(0, chips - 1)], r2s.at[n]))
+
+    def late_spread(n):
+        settle(er.at[n, pl.ds(0, chips - 1)], r2r.at[n])
+        mine = rr.at[n, c * ncrs + b]
+        rr[n, c * ncrs + b] = jnp.sum(er[n], axis=0)
+        for cc in range(2):
+            for j in range(ncrs):
+                if cc == 0 and j == 0:
+                    continue
+                dev = (a if cc == 0 else sib, lax.rem(b + j, ncrs))
+                remote(mine, mine, r1s.at[n], r1r.at[n], dev).start()
+        drains.append(lambda: settle(rr.at[n, pl.ds(0, 2 * ncrs - 1)], r1s.at[n]))
+
+    def late_end(n):
+        settle(rr.at[n, pl.ds(0, 2 * ncrs - 1)], r1r.at[n])
+        total = jnp.sum(rr[n], axis=0)
+        return total[0:ncrs], total[ncrs:]
+
     def faces_start(n, which):
         copies = []
         for pos in which:
@@ -313,7 +342,31 @@
         x3[NX + lo:NX + lo + FACE, :] = low
         x3[2 * NX + lo:2 * NX + lo + FACE, :] = high
 
-    pbuf[0, 0:NC] = apply_loads(0, NC)
+    both = dot(jnp.concatenate([a0hi[0:NC, :], a0lo[0:NC, :]], axis=0), lhi[...])
+    pbuf[0, 0:NC] = both[0:NC] + both[NC:] + dot(a0hi[0:NC, :], llo[...])
+    pl.semaphore_wait(barrier, greeted)
+    coarse_begin(0, (0, 1))
+
+    in_copies[1].wait()
+    cip[0:cblock, 0:ncoarse] = civ[...]
+    high, low = split(cip[...])
+    i = cols_of((1, cbp))
+    r = cblock * b + i
+    plane = div(r, 24)
+    base = lax.div(lax.div(cblock * b, 24), 2)
+    target = 24 * ((plane >> 1) - base) + r - 24 * plane
+    target = jnp.where((((plane + 1) & 1) == c) & (i < cblock), target, -1)
+    pct = hot(target == rows_of((LANES, cbp)))
+    x1h = dot(pct, high).astype(BF16)
+    x1l = dot(pct, low).astype(BF16)
+    i = rows_of((LANES, 1))
+    r = 48 * k - 48 + i
+    r = jnp.where((i < 120) & (r < ncoarse), r, -1)
+    sel = hot(r == cols_of((LANES, ncp)))
+    dall[b] = dot_nt(sel, x1h) + dot_nt(sel, x1l)
+    for j in range(1, ncrs):
+        remote(dall.at[b], dall.at[b], csend.at[j], crecv.at[j], (a, lax.rem(b + j, ncrs))).start()
+
     bch = dot_nt(bmat[...], chi).astype(BF16)
     bcl = dot_nt(bmat[...], clo).astype(BF16)
     l = rows_of((32, 1))
@@ -331,24 +384,9 @@
         ws[band, :] = dot(bch[band], emaps[pos - 1]) + dot(bcl[band], emaps[pos - 1])
     wcopies = [remote(ws.at[pl.ds(pos * FACE, FACE)], wr.at[pl.ds((pos ^ 1) * FACE, FACE)],
                       wsend.at[pos], wrecv.at[pos ^ 1], dests[pos]) for pos in range(4)]
-
-    in_copies[1].wait()
-    cip[0:cblock, 0:ncoarse] = civ[...]
-    high, low = split(cip[...])
-    i = cols_of((1, cbp))
-    r = cblock * b + i
-    plane = div(r, 24)
-    base = lax.div(lax.div(cblock * b, 24), 2)
-    target = 24 * ((plane >> 1) - base) + r - 24 * plane
-    target = jnp.where((((plane + 1) & 1) == c) & (i < cblock), target, -1)
-    pct = hot(target == rows_of((LANES, cbp)))
-    x1h = dot(pct, high).astype(BF16)
-    x1l = dot(pct, low).astype(BF16)
-    i = rows_of((LANES, 1))
-    r = 48 * k - 48 + i
-    r = jnp.where((i < 120) & (r < ncoarse), r, -1)
-    sel = hot(r == cols_of((LANES, ncp)))
-    dall[b] = dot_nt(sel, x1h) + dot_nt(sel, x1l)
+    for copy in wcopies:
+        copy.start()
+
     in_copies[3].wait()
 
     def split_k(i, carry):
@@ -375,12 +413,6 @@
 
     half = 2 * FACE
     face_rows(0, half)
-    pl.semaphore_wait(barrier, greeted)
-    coarse_begin(0, (0, 1))
-    for copy in wcopies:
-        copy.start()
-    for j in range(1, ncrs):
-        remote(dall.at[b], dall.at[b], csend.at[j], crecv.at[j], (a, lax.rem(b + j, ncrs))).start()
     tb[0, 0:half, :] = apply_loads(NC, NC + half)
     copies = faces_start(0, (0, 1))
     face_rows(half, NX)
@@ -417,21 +449,15 @@
         a3[at, 2 * NX:] = dot(a0lo[src, :], bmt[...]).astype(BF16)
         return carry
 
-    lax.fori_loop(0, 2, between, 0)
     coarse_copy = coarse_solve(0)
 
-    in_copies[4].wait()
-    nface = sv.shape[0]
-    sp[0:nface, 0:nface] = sv[...]
+    nface = sv.shape[2]
+    for pos in range(4):
+        in_copies[4 + pos].wait()
+        sp[pos * FACE:pos * FACE + fdof, 0:nface] = sv[pos] * (0.5 if pos % 2 else -0.5)
     high, low = split(sp[...])
     khi[0:NX, 0:NX] = high
     klo[0:NX, 0:NX] = low
-    for pos in range(4):
-        face = ORDER[pos]
-        sign = 0.5 if pos % 2 else -0.5
-        j = rows_of((FACE, 1))
-        target = jnp.where(j < fdof, j + face * fdof, -1)
-        tmat[pos * FACE:(pos + 1) * FACE, :] = hot(target == cols_of((FACE, NX)), sign)
     pos_l = jnp.where(lane >= FACE, 1, 0) + jnp.where(lane >= 2 * FACE, 1, 0) + jnp.where(lane >= 3 * FACE, 1, 0)
     j = lane - FACE * pos_l
     target = jnp.where(j < fdof, j + fdof * ((pos_l + 2) & 3), -1)
@@ -440,9 +466,8 @@
 
     def precond_rows(i, carry):
         at = pl.ds(pl.multiple_of(i * FACE, FACE), FACE)
-        high = dot(tmat[at, :], khi[0:NX, 0:NX]).astype(BF16)
-        low = dot(tmat[at, :], klo[0:NX, 0:NX]).astype(BF16)
-        high = dot(high, tmt[...]).astype(BF16)
+        high = dot(khi[at, 0:NX], tmt[...]).astype(BF16)
+        low = klo[at, 0:NX]
         to = pl.ds(pl.multiple_of(NW + i * FACE, 16), FACE)
         m3[to, 0:NX] = high
         m3[to, NX:2 * NX] = high
@@ -466,7 +491,8 @@
     w3[:, 2 * LANES:] = low
     high, low = split(jnp.transpose(wo[...]))
     mhi, mlo = m3[NW:, 0:NX], m3[NW:, 2 * NX:]
-    high, low = split((dot(high, mhi) + dot(high, mlo) + dot(low, mhi))[0:NW])
+    both = dot(jnp.concatenate([high[0:NW], low[0:NW]], axis=0), mhi)
+    high, low = split(both[0:NW] + both[NW:] + dot(high[0:NW], mlo))
     m3[0:NW, 0:NX] = high
     m3[0:NW, NX:2 * NX] = high
     m3[0:NW, 2 * NX:] = low
@@ -485,7 +511,7 @@
 
     around = (-1, 0, 1, 2)
 
-    def precond(n, f, total):
+    def precond(n, f, total, idle):
         block = dot(m3[0:NW + half, :], x3[...])
         pbuf[f] = block[0:NW]
         coarse_begin(f, around)
@@ -500,21 +526,22 @@
         if total is not None:
             sum_begin(total, rz_part, jnp.zeros((ncrs, LANES), F32))
             copies += faces_start(n, (0, 1, 2, 3))
+            sum_gather(total)
         coarse_gather(f, around)
-        if total is not None:
-            sum_gather(total)
-        coarse_copy = coarse_solve(f)
+        idle()
         faces_wait(copies)
-        return coarse_copy, rz_part
+        return rz_part
 
     def operator(n, f, rz_part, scale):
         tb[n % 2, 0:half, :] = dot(a3[0:half, :], x3[...])
+        copies = faces_start(n, (0, 1))
         tb[n % 2, half:, :] = dot(a3[half:, :], x3[...])
+        copies += faces_start(n, (2, 3))
         energy = packed(jnp.sum(dv[...] * tb[n % 2], axis=0, keepdims=True))
+        coarse_spread(f, coarse_solve(f))
         energy = energy + jnp.where(rows_of((ncrs, LANES)) == b, coarse_energy(f, scale), 0.0)
-        sum_begin(f, rz_part, energy)
-        copies = faces_start(n, (0, 1, 2, 3))
-        sum_gather(f)
+        late_begin(f, rz_part, energy)
+        late_spread(f)
         return copies
 
     def keep_image(n):
@@ -522,16 +549,15 @@
             tb[n % 2, pos * FACE:(pos + 1) * FACE, :] = value
         return use
 
-    coarse_copy, rz_part = precond(1, 1, None)
+    rz_part = precond(1, 1, None, lambda: lax.fori_loop(0, 2, between, 0))
     for pos in range(4):
         value = jumped(1, pos)
         dv[pos * FACE:(pos + 1) * FACE, :] = value
         put_x(pos, value)
 
-    coarse_spread(1, coarse_copy)
     copies = operator(2, 1, rz_part, None)
     operator_end(2, 1, copies, keep_image(2))
-    rz_now, energy = sum_end(1)
+    rz_now, energy = late_end(1)
     alpha = unpacked(rz_now / energy)
     for pos in range(4):
         band = slice(pos * FACE, (pos + 1) * FACE)
@@ -539,11 +565,12 @@
         rv[band, :] = value
         put_x(pos, value)
 
-    coarse_copy, rz_part = precond(3, 2, 0)
-    coarse_spread(2, coarse_copy)
-    for pos in range(4):
-        band = slice(pos * FACE, (pos + 1) * FACE)
-        mv[band, :] = alpha * dv[band, :]
+    def first_multipliers():
+        for pos in range(4):
+            band = slice(pos * FACE, (pos + 1) * FACE)
+            mv[band, :] = alpha * dv[band, :]
+
+    rz_part = precond(3, 2, 0, first_multipliers)
     rz_next, _ = sum_end(0)
     beta = unpacked(rz_next / rz_now)
     co[0:1, :] = beta
@@ -555,7 +582,7 @@
 
     copies = operator(4, 2, rz_next, co)
     operator_end(4, 2, copies, keep_image(4), co)
-    _, energy = sum_end(2)
+    _, energy = late_end(2)
     alpha = unpacked(rz_next / energy)
     out_copies = []
     for pos in range(4):
@@ -588,7 +615,7 @@
     vm = pltpu.VMEM
     dma = pltpu.SemaphoreType.DMA
     scratch = [
-        vm((nrows, nrows), F32), vm((nrows, cases), F32), vm((ncl, nrows), F32), vm((nface, nface), F32),
+        vm((nrows, nrows), F32), vm((nrows, cases), F32), vm((ncl, nrows), F32), vm((4, fdof, nface), F32),
         vm(coarse_inverse.shape, F32),
         vm((nrp, nrp), BF16), vm((nrp, nrp), BF16), vm((16, nrp), F32),
         vm((8, NX), jnp.int32), vm((NX, 8), jnp.int32),
@@ -596,7 +623,7 @@
         vm((nrp, cases), BF16), vm((nrp, cases), BF16),
         vm((NX, 3 * NX), BF16), vm((NW + NX, 3 * NX), BF16), vm((NX, 3 * LANES), BF16), vm((3 * NX, cases), BF16),
         vm((32, nrp), F32), vm((cbp, ncp), F32),
-        vm((NX, NX), F32), vm((NX, NX), BF16), vm((NX, NX), BF16),
+        vm((NX, NX), F32), vm((NX, NX), BF16),
         vm((NX, LANES), F32), vm((NX, LANES), F32), vm((NX, LANES), F32),
         vm((ncrs, LANES, LANES), F32), vm((LANES, chips * 24), BF16), vm((LANES, chips * 24), BF16),
         vm((2, NX, cases), F32), vm((2, 4, FACE, cases), F32),
@@ -606,7 +633,7 @@
         vm((2, 24, LANES), F32), vm((3, LANES, cases), F32), vm((3 * LANES, cases), BF16),
         vm((3, 8, LANES), F32), vm((3, 2 * ncrs, 8, LANES), F32), vm((3, chips, 8, LANES), F32),
         vm((8, cases), F32), vm((8, fdof, cases), F32),
-        dma((5,)), dma((8,)), dma((2, 4)), dma((2, 4)), dma((4,)), dma((4,)), dma((ncrs,)), dma((ncrs,)),
+        dma((8,)), dma((8,)), dma((2, 4)), dma((2, 4)), dma((4,)), dma((4,)), dma((ncrs,)), dma((ncrs,)),
     ] + [dma((3,)) for _ in range(12)]
     out = jax.ShapeDtypeStruct((1, fdof, 4, cases), F32)
     anyspace = pl.BlockSpec(memory_space=pl.ANY)

time: 94.2 us -> 90 us (0.955)
  Pallas kernels: 89.7 us -> 85.5 us
    pallas_call x1, Pallas kernels: 89.7 us -> 85.5 us  [body(): pl.pallas_call(functools.partial(kernel, dims), out_shape=(out, out), in_...]
where the time goes in v4:
time: 90 us; the launch traced here: 89.8 us
  Pallas kernels  85.5 us (95%)
  local copies, waits for them, and re-layouts  3.63 us (4%)
    pallas_call x1, Pallas kernels, body(): pl.pallas_call(functools.partial(kernel, dims), out_shape=(out, out), in_...  85.5 us
    unnamed x4, local copies, waits for them, and re-layouts  3.63 us

profile of v4, /device:TPU:1, one launch (start us, length us, event | category | flops | bytes accessed | tf_op | source)
XLA Modules:
  0.0 89.8 jit_solution(7365844940985141879)
XLA Ops:
  0.6 85.5 %shard_map.77 = (f32[1,147,4,512]{3,2,1,0:T(4,128)}, f32[1,147,4,512]{3,2,1,0:T(4,128)}) custom-call(s32[1,4,147]{2,1,0:T(4,128)} %faces.1, f32[1215,1,1215]{2,1,0:T(1,128)} %bitcast.6, f32[588,1,588]{2,1,0:T(1,128)} %bitcast.8, f32[1,24,1215]{2,1,0:T(8,128)} %bitcast.11, f32[186,744]{1,0:T(8,128)} %cinv.1, f32[1215,1,512]{2,1,0:T(1,128)} %bitcast.7), custom_call_target="tpu_custom_call" | custom-call | tf_op jit(solution)/shard_map/pallas_call | solution.py:642
  86.2 0.0 copy-start
  86.2 2.6 %copy.10 = f32[1,4,147,512]{3,1,2,0:T(4,128)} copy(f32[1,4,147,512]{3,1,2,0:T(4,128)} %bitcast.10) | data formatting | bytes 2408448
  88.8 0.0 copy-done
  88.8 1.0 %copy.11 = f32[1,4,147,512]{3,1,2,0:T(4,128)} copy(f32[1,4,147,512]{3,1,2,0:T(4,128)S(1)} %bitcast.9) | data formatting | bytes 2408448
Async XLA Ops:
  86.2 2.6 %copy-start = (f32[1,147,4,512]{3,2,1,0:T(4,128)S(1)}, f32[1,147,4,512]{3,2,1,0:T(4,128)}, u32[]{:S(2)}) copy-start(f32[1,147,4,512]{3,2,1,0:T(4,128)} %get-tuple-element.5) | copy-start | bytes 3612676

commit v5 on v4

--- a/solution.py
+++ b/solution.py
@@ -53,10 +53,10 @@
 def kernel(dims, faces, kinv, schur, corner, cinv, loads, mo, ro,
            kv, lv, cv, sv, civ, khi, klo, tail, idxr, idxc, bmat, bmt, a0hi, a0lo, lhi, llo, a3, m3, w3, x3,
            cpad, cip, sp, tmt, ws, wo, wr, dall, dphi, dplo,
-           tb, rb, rv, dv, mv, pbuf, p0, gb, sibs, sibr, hs, hk, qk, hb, h3,
-           rs, rr, er, co, outs,
+           tb, rb, rv, dv, mv, zv, tk, wv, pbuf, p0, gb, sibs, sibr, hs, hk, qk, hb, h3,
+           qs, rr, er, co, outs,
            dsem, osem, fsend, frecv, wsend, wrecv, csend, crecv,
-           s1s, s1r, s2s, s2r, bs, br, s3s, s3r, r1s, r1r, r2s, r2r):
+           s1s, s1r, s2s, s2r, bs, br, s3s, s3r, r1s, r1r, r2s, r2r, qsend, qrecv):
     nsub, ncrs, nrows, fdof, cases, ncoarse = dims
     chips = nsub // 2
     nrp = khi.shape[1]
@@ -202,13 +202,16 @@
             return carry
 
         lax.fori_loop(1, chips, send, 0)
+        other = remote(gb.at[f, k], qs.at[f], qsend.at[f], qrecv.at[f], (sib, b))
+        other.start()
         drains.append(lambda: settle(gb.at[f, pl.ds(0, chips - 1)], s2s.at[f]))
+        drains.append(other.wait_send)
+        return other
 
     def coarse_solve(f):
         settle(gb.at[f, pl.ds(0, chips - 1)], s2r.at[f])
         high, low = split(gb[f].reshape(chips * 24, LANES))
-        sibs[f, 0:LANES] = dot(dphi[...], high) + dot(dphi[...], low) + dot(dplo[...], high)
-        sibs[f, LANES:LANES + 24] = gb[f, k]
+        sibs[f] = dot(dphi[...], high) + dot(dphi[...], low) + dot(dplo[...], high)
         copy = remote(sibs.at[f], sibr.at[f], bs.at[f], br.at[f], (sib, b))
         copy.start()
         return copy
@@ -216,17 +219,17 @@
     def coarse_spread(f, copy):
         copy.wait()
         at = pl.ds(pl.multiple_of(b * LANES, LANES), LANES)
-        total = sibs[f, 0:LANES] + sibr[f, 0:LANES]
-        hs[...] = total
+        hs[...] = sibs[f] + sibr[f]
         hb[f, 0:NW, at] = hs[pl.ds(pl.multiple_of(24 * c, 8), NW), :]
         for j in range(1, ncrs):
             remote(hb.at[f, pl.ds(0, NW), at], hb.at[f, pl.ds(0, NW), at], s3s.at[f], s3r.at[f],
                    (a, lax.rem(b + j, ncrs))).start()
         drains.append(lambda: settle(hb.at[f, pl.ds(0, NW), pl.ds(0, (ncrs - 1) * LANES)], s3s.at[f]))
 
-    def coarse_energy(f, scale=None):
+    def coarse_energy(f, qcopy, scale=None):
         at = pl.ds(pl.multiple_of(b * LANES, LANES), LANES)
-        total, mine, other = hs[...], sibs[f, LANES:LANES + 24], sibr[f, LANES:LANES + 24]
+        qcopy.wait_recv()
+        total, mine, other = sibs[f], gb[f, k], qs[f]
         if scale is not None:
             part = scale[0:1, at]
             total = total + part * hk[...]
@@ -237,14 +240,11 @@
         qk[1] = other
         mine = hk[pl.ds(pl.multiple_of(24 + 24 * c, 8), 24), :] * mine
         other = hk[pl.ds(pl.multiple_of(48 - 24 * c, 8), 24), :] * other
-        return 0.5 * jnp.sum(mine + other, axis=0, keepdims=True)
-
-    def coarse_end(f, scale=None):
-        settle(hb.at[f, pl.ds(0, 96), pl.ds(0, (ncrs - 1) * LANES)], s3r.at[f])
-        value = hb[f]
-        if scale is not None:
-            value = value + scale[0:1, :] * hb[f - 1]
-        high, low = split(value)
+        return jnp.sum(mine + other, axis=0, keepdims=True)
+
+    def coarse_end(f):
+        settle(hb.at[f, pl.ds(0, NW), pl.ds(0, (ncrs - 1) * LANES)], s3r.at[f])
+        high, low = split(hb[f])
         h3[0:LANES, :] = high
         h3[LANES:2 * LANES, :] = low
         h3[2 * LANES:, :] = high
@@ -256,34 +256,6 @@
 
     def unpacked(value):
         return jnp.concatenate([value[i:i + 1] for i in range(ncrs)], axis=1)
-
-    def sum_begin(n, first, second):
-        rs[n] = jnp.concatenate([first, second], axis=0)
-        for cc in range(2):
-            for j in range(ncrs):
-                if cc == 0 and j == 0:
-                    rr[n, c * ncrs + b] = rs[n]
-                    continue
-                dev = (a if cc == 0 else sib, lax.rem(b + j, ncrs))
-                remote(rs.at[n], rr.at[n, c * ncrs + b], r1s.at[n], r1r.at[n], dev).start()
-        drains.append(lambda: settle(rr.at[n, pl.ds(0, 2 * ncrs - 1)], r1s.at[n]))
-
-    def sum_gather(n):
-        settle(rr.at[n, pl.ds(0, 2 * ncrs - 1)], r1r.at[n])
-        er[n, k] = jnp.sum(rr[n], axis=0)
-
-        def send(j, carry):
-            to = 2 * lax.rem(k + j, chips) + c
-            remote(er.at[n, k], er.at[n, k], r2s.at[n], r2r.at[n], (to, b)).start()
-            return carry
-
-        lax.fori_loop(1, chips, send, 0)
-        drains.append(lambda: settle(er.at[n, pl.ds(0, chips - 1)], r2s.at[n]))
-
-    def sum_end(n):
-        settle(er.at[n, pl.ds(0, chips - 1)], r2r.at[n])
-        total = jnp.sum(er[n], axis=0)
-        return total[0:ncrs], total[ncrs:]
 
     def late_begin(n, first, second):
         er[n, k] = jnp.concatenate([first, second], axis=0)
@@ -313,11 +285,12 @@
         total = jnp.sum(rr[n], axis=0)
         return total[0:ncrs], total[ncrs:]
 
-    def faces_start(n, which):
+    def faces_start(n, which, lanes=slice(0, cases), h=0):
         copies = []
+        at = pl.ds(lanes.start, lanes.stop - lanes.start)
         for pos in which:
-            copy = remote(tb.at[n % 2, pl.ds(pos * FACE, SENT)], rb.at[n % 2, pos ^ 1, pl.ds(0, SENT)],
-                          fsend.at[n % 2, pos], frecv.at[n % 2, pos ^ 1], dests[pos])
+            copy = remote(tb.at[n % 2, pl.ds(pos * FACE, SENT), at], rb.at[n % 2, pos ^ 1, pl.ds(0, SENT), at],
+                          fsend.at[2 * (n % 2) + h, pos], frecv.at[2 * (n % 2) + h, pos ^ 1], dests[pos])
             copy.start()
             copies.append(copy)
         return copies
@@ -326,21 +299,21 @@
         for copy in copies:
             copy.wait()
 
-    def jumped(n, pos, extra=None):
-        band = slice(pos * FACE, (pos + 1) * FACE)
-        value = tb[n % 2, band, :] + rb[n % 2, pos]
+    def jumped(n, pos, extra=None, lanes=slice(0, cases)):
+        band = slice(pos * FACE, (pos + 1) * FACE)
+        value = tb[n % 2, band, lanes] + rb[n % 2, pos, :, lanes]
         if extra is not None:
             value = value + extra
         if keeps[pos] is not None:
             value = jnp.where(keeps[pos], value, 0.0)
         return value
 
-    def put_x(pos, value):
+    def put_x(pos, value, lanes=slice(0, cases)):
         high, low = split(value)
         lo = pos * FACE
-        x3[lo:lo + FACE, :] = high
-        x3[NX + lo:NX + lo + FACE, :] = low
-        x3[2 * NX + lo:2 * NX + lo + FACE, :] = high
+        x3[lo:lo + FACE, lanes] = high
+        x3[NX + lo:NX + lo + FACE, lanes] = low
+        x3[2 * NX + lo:2 * NX + lo + FACE, lanes] = high
 
     both = dot(jnp.concatenate([a0hi[0:NC, :], a0lo[0:NC, :]], axis=0), lhi[...])
     pbuf[0, 0:NC] = both[0:NC] + both[NC:] + dot(a0hi[0:NC, :], llo[...])
@@ -416,7 +389,7 @@
     tb[0, 0:half, :] = apply_loads(NC, NC + half)
     copies = faces_start(0, (0, 1))
     face_rows(half, NX)
-    coarse_gather(0, (0, 1))
+    qcopy = coarse_gather(0, (0, 1))
     tb[0, half:NX, :] = apply_loads(NC + half, NC + NX)
     copies += faces_start(0, (2, 3))
 
@@ -475,6 +448,7 @@
         return carry
 
     coarse_spread(0, coarse_copy)
+    qcopy.wait_recv()
     lax.fori_loop(0, 4, precond_rows, 0)
 
     for copy in wcopies:
@@ -497,8 +471,8 @@
     m3[0:NW, NX:2 * NX] = high
     m3[0:NW, 2 * NX:] = low
 
-    def operator_end(n, f, copies, use, scale=None):
-        coarse_end(f, scale)
+    def operator_end(n, f, copies, use):
+        coarse_end(f)
         faces_wait(copies)
         for pos in range(4):
             use(pos, jumped(n, pos, dot(w3[pos * FACE:(pos + 1) * FACE, :], h3[...])))
@@ -511,84 +485,93 @@
 
     around = (-1, 0, 1, 2)
 
-    def precond(n, f, total, idle):
+    halves = (slice(0, cases // 2), slice(cases // 2, cases))
+    every = (0, 1, 2, 3)
+
+    def precond(n, f):
         block = dot(m3[0:NW + half, :], x3[...])
         pbuf[f] = block[0:NW]
         coarse_begin(f, around)
         tb[n % 2, 0:half, :] = block[NW:]
-        copies = []
-        if total is None:
-            copies += faces_start(n, (0, 1))
         tb[n % 2, half:, :] = dot(m3[NW + half:, :], x3[...])
-        if total is None:
-            copies += faces_start(n, (2, 3))
-        rz_part = packed(jnp.sum(rv[...] * tb[n % 2], axis=0, keepdims=True))
-        if total is not None:
-            sum_begin(total, rz_part, jnp.zeros((ncrs, LANES), F32))
-            copies += faces_start(n, (0, 1, 2, 3))
-            sum_gather(total)
-        coarse_gather(f, around)
-        idle()
-        faces_wait(copies)
-        return rz_part
-
-    def operator(n, f, rz_part, scale):
-        tb[n % 2, 0:half, :] = dot(a3[0:half, :], x3[...])
-        copies = faces_start(n, (0, 1))
-        tb[n % 2, half:, :] = dot(a3[half:, :], x3[...])
-        copies += faces_start(n, (2, 3))
-        energy = packed(jnp.sum(dv[...] * tb[n % 2], axis=0, keepdims=True))
-        coarse_spread(f, coarse_solve(f))
-        energy = energy + jnp.where(rows_of((ncrs, LANES)) == b, coarse_energy(f, scale), 0.0)
+        return [faces_start(n, every, lanes, h) for h, lanes in enumerate(halves)]
+
+    def operator(n, copies, keep_z):
+        out = []
+        for h, lanes in enumerate(halves):
+            faces_wait(copies[h])
+            for pos in range(4):
+                value = jumped(n - 1, pos, None, lanes)
+                keep_z[pos * FACE:(pos + 1) * FACE, lanes] = value
+                put_x(pos, value, lanes)
+            tb[n % 2, 0:half, lanes] = dot(a3[0:half, :], x3[:, lanes])
+            tb[n % 2, half:, lanes] = dot(a3[half:, :], x3[:, lanes])
+            out += faces_start(n, every, lanes, h)
+        return out
+
+    def operator_sums(f, qcopy, rz_part, energy, scale):
+        coarse_copy = coarse_solve(f)
+        energy = energy + jnp.where(rows_of((ncrs, LANES)) == b, coarse_energy(f, qcopy, scale), 0.0)
         late_begin(f, rz_part, energy)
+        coarse_spread(f, coarse_copy)
         late_spread(f)
-        return copies
-
-    def keep_image(n):
-        def use(pos, value):
-            tb[n % 2, pos * FACE:(pos + 1) * FACE, :] = value
-        return use
-
-    rz_part = precond(1, 1, None, lambda: lax.fori_loop(0, 2, between, 0))
-    for pos in range(4):
-        value = jumped(1, pos)
-        dv[pos * FACE:(pos + 1) * FACE, :] = value
-        put_x(pos, value)
-
-    copies = operator(2, 1, rz_part, None)
-    operator_end(2, 1, copies, keep_image(2))
+
+    def total_rz(n):
+        return packed(jnp.sum(rv[...] * tb[n % 2], axis=0, keepdims=True))
+
+    copies = precond(1, 1)
+    rz_part = total_rz(1)
+    lax.fori_loop(0, 2, between, 0)
+    qcopy = coarse_gather(1, around)
+
+    copies = operator(2, copies, dv)
+    tk[...] = tb[0]
+    operator_sums(1, qcopy, rz_part, packed(jnp.sum(dv[...] * tk[...], axis=0, keepdims=True)), None)
+
+    def keep_image(pos, value):
+        wv[pos * FACE:(pos + 1) * FACE, :] = value
+
+    operator_end(2, 1, copies, keep_image)
     rz_now, energy = late_end(1)
     alpha = unpacked(rz_now / energy)
     for pos in range(4):
         band = slice(pos * FACE, (pos + 1) * FACE)
-        value = rv[band, :] - alpha * tb[0, band, :]
+        value = rv[band, :] - alpha * wv[band, :]
         rv[band, :] = value
         put_x(pos, value)
 
-    def first_multipliers():
-        for pos in range(4):
-            band = slice(pos * FACE, (pos + 1) * FACE)
-            mv[band, :] = alpha * dv[band, :]
-
-    rz_part = precond(3, 2, 0, first_multipliers)
-    rz_next, _ = sum_end(0)
+    copies = precond(3, 2)
+    late_begin(0, total_rz(3), jnp.zeros((ncrs, LANES), F32))
+    for pos in range(4):
+        band = slice(pos * FACE, (pos + 1) * FACE)
+        mv[band, :] = alpha * dv[band, :]
+    qcopy = coarse_gather(2, around)
+    late_spread(0)
+
+    copies = operator(4, copies, zv)
+    rz_next, _ = late_end(0)
     beta = unpacked(rz_next / rz_now)
     co[0:1, :] = beta
-    for pos in range(4):
-        band = slice(pos * FACE, (pos + 1) * FACE)
-        value = jumped(3, pos) + beta * dv[band, :]
+    parts = 0.0
+    for pos in range(4):
+        band = slice(pos * FACE, (pos + 1) * FACE)
+        value = zv[band, :] + beta * dv[band, :]
         dv[band, :] = value
-        put_x(pos, value)
-
-    copies = operator(4, 2, rz_next, co)
-    operator_end(4, 2, copies, keep_image(4), co)
+        parts = parts + jnp.sum(value * (tb[0, band, :] + beta * tk[band, :]), axis=0, keepdims=True)
+    operator_sums(2, qcopy, jnp.zeros((ncrs, LANES), F32), packed(parts), co)
+
+    def whole_image(pos, value):
+        band = slice(pos * FACE, (pos + 1) * FACE)
+        wv[band, :] = value + beta * wv[band, :]
+
+    operator_end(4, 2, copies, whole_image)
     _, energy = late_end(2)
     alpha = unpacked(rz_next / energy)
     out_copies = []
     for pos in range(4):
         band = slice(pos * FACE, (pos + 1) * FACE)
         outs[pos] = (mv[band, :] + alpha * dv[band, :])[0:fdof]
-        outs[4 + pos] = (rv[band, :] - alpha * tb[0, band, :])[0:fdof]
+        outs[4 + pos] = (rv[band, :] - alpha * wv[band, :])[0:fdof]
         for side, ref in enumerate((mo, ro)):
             copy = pltpu.make_async_copy(outs.at[4 * side + pos], ref.at[0, :, ORDER[pos]], osem.at[4 * side + pos])
             copy.start()
@@ -628,13 +611,14 @@
         vm((ncrs, LANES, LANES), F32), vm((LANES, chips * 24), BF16), vm((LANES, chips * 24), BF16),
         vm((2, NX, cases), F32), vm((2, 4, FACE, cases), F32),
         vm((NX, cases), F32), vm((NX, cases), F32), vm((NX, cases), F32),
+        vm((NX, cases), F32), vm((NX, cases), F32), vm((NX, cases), F32),
         vm((3, NW, cases), F32), vm((3, 4 * ncrs, 24, LANES), F32), vm((3, chips, 24, LANES), F32),
-        vm((3, LANES + 24, LANES), F32), vm((3, LANES + 24, LANES), F32), vm((LANES, LANES), F32), vm((LANES, LANES), F32),
+        vm((3, LANES, LANES), F32), vm((3, LANES, LANES), F32), vm((LANES, LANES), F32), vm((LANES, LANES), F32),
         vm((2, 24, LANES), F32), vm((3, LANES, cases), F32), vm((3 * LANES, cases), BF16),
-        vm((3, 8, LANES), F32), vm((3, 2 * ncrs, 8, LANES), F32), vm((3, chips, 8, LANES), F32),
+        vm((3, 24, LANES), F32), vm((3, 2 * ncrs, 8, LANES), F32), vm((3, chips, 8, LANES), F32),
         vm((8, cases), F32), vm((8, fdof, cases), F32),
-        dma((8,)), dma((8,)), dma((2, 4)), dma((2, 4)), dma((4,)), dma((4,)), dma((ncrs,)), dma((ncrs,)),
-    ] + [dma((3,)) for _ in range(12)]
+        dma((8,)), dma((8,)), dma((4, 4)), dma((4, 4)), dma((4,)), dma((4,)), dma((ncrs,)), dma((ncrs,)),
+    ] + [dma((3,)) for _ in range(14)]
     out = jax.ShapeDtypeStruct((1, fdof, 4, cases), F32)
     anyspace = pl.BlockSpec(memory_space=pl.ANY)
     inside = pl.BlockSpec(memory_space=pltpu.VMEM)

time: 90 us -> 86.9 us (0.966)
  Pallas kernels: 85.5 us -> 82.4 us
    pallas_call x1, Pallas kernels: 85.5 us -> 82.4 us  [body(): pl.pallas_call(functools.partial(kernel, dims), out_shape=(out, out), in_...]
where the time goes in v5:
time: 86.9 us; the launch traced here: 86.7 us
  Pallas kernels  82.4 us (95%)
  local copies, waits for them, and re-layouts  3.63 us (4%)
    pallas_call x1, Pallas kernels, body(): pl.pallas_call(functools.partial(kernel, dims), out_shape=(out, out), in_...  82.4 us
    unnamed x4, local copies, waits for them, and re-layouts  3.63 us

profile of v5, /device:TPU:1, one launch (start us, length us, event | category | flops | bytes accessed | tf_op | source)
XLA Modules:
  0.0 86.7 jit_solution(1261236486256829697)
XLA Ops:
  0.6 82.4 %shard_map.77 = (f32[1,147,4,512]{3,2,1,0:T(4,128)}, f32[1,147,4,512]{3,2,1,0:T(4,128)}) custom-call(s32[1,4,147]{2,1,0:T(4,128)} %faces.1, f32[1215,1,1215]{2,1,0:T(1,128)} %bitcast.6, f32[588,1,588]{2,1,0:T(1,128)} %bitcast.8, f32[1,24,1215]{2,1,0:T(8,128)} %bitcast.11, f32[186,744]{1,0:T(8,128)} %cinv.1, f32[1215,1,512]{2,1,0:T(1,128)} %bitcast.7), custom_call_target="tpu_custom_call" | custom-call | tf_op jit(solution)/shard_map/pallas_call | solution.py:626
  83.0 0.0 copy-start
  83.1 2.6 %copy.10 = f32[1,4,147,512]{3,1,2,0:T(4,128)} copy(f32[1,4,147,512]{3,1,2,0:T(4,128)} %bitcast.10) | data formatting | bytes 2408448
  85.7 0.0 copy-done
  85.7 1.0 %copy.11 = f32[1,4,147,512]{3,1,2,0:T(4,128)} copy(f32[1,4,147,512]{3,1,2,0:T(4,128)S(1)} %bitcast.9) | data formatting | bytes 2408448
Async XLA Ops:
  83.0 2.6 %copy-start = (f32[1,147,4,512]{3,2,1,0:T(4,128)S(1)}, f32[1,147,4,512]{3,2,1,0:T(4,128)}, u32[]{:S(2)}) copy-start(f32[1,147,4,512]{3,2,1,0:T(4,128)} %get-tuple-element.5) | copy-start | bytes 3612676

commit v6 on v5

--- a/solution.py
+++ b/solution.py
@@ -50,11 +50,11 @@
     return (value * (65536 // by + 1)) >> 16
 
 
-def kernel(dims, faces, kinv, schur, corner, cinv, loads, mo, ro,
+def kernel(dims, faces, kinv, schur, corner, cinv, loads, mo, do, ro, wo_out, alpha_out,
            kv, lv, cv, sv, civ, khi, klo, tail, idxr, idxc, bmat, bmt, a0hi, a0lo, lhi, llo, a3, m3, w3, x3,
            cpad, cip, sp, tmt, ws, wo, wr, dall, dphi, dplo,
            tb, rb, rv, dv, mv, zv, tk, wv, pbuf, p0, gb, sibs, sibr, hs, hk, qk, hb, h3,
-           qs, rr, er, co, outs,
+           qs, rr, er, co,
            dsem, osem, fsend, frecv, wsend, wrecv, csend, crecv,
            s1s, s1r, s2s, s2r, bs, br, s3s, s3r, r1s, r1r, r2s, r2r, qsend, qrecv):
     nsub, ncrs, nrows, fdof, cases, ncoarse = dims
@@ -388,8 +388,8 @@
     face_rows(0, half)
     tb[0, 0:half, :] = apply_loads(NC, NC + half)
     copies = faces_start(0, (0, 1))
+    qcopy = coarse_gather(0, (0, 1))
     face_rows(half, NX)
-    qcopy = coarse_gather(0, (0, 1))
     tb[0, half:NX, :] = apply_loads(NC + half, NC + NX)
     copies += faces_start(0, (2, 3))
 
@@ -519,6 +519,12 @@
     def total_rz(n):
         return packed(jnp.sum(rv[...] * tb[n % 2], axis=0, keepdims=True))
 
+    def leave(src, dst, n):
+        for pos in range(4):
+            copy = pltpu.make_async_copy(src.at[pl.ds(pos * FACE, SENT)], dst.at[0, :, ORDER[pos]], osem.at[4 * n + pos])
+            copy.start()
+            drains.append(copy.wait)
+
     copies = precond(1, 1)
     rz_part = total_rz(1)
     lax.fori_loop(0, 2, between, 0)
@@ -545,6 +551,8 @@
     for pos in range(4):
         band = slice(pos * FACE, (pos + 1) * FACE)
         mv[band, :] = alpha * dv[band, :]
+    leave(rv, ro, 0)
+    leave(mv, mo, 1)
     qcopy = coarse_gather(2, around)
     late_spread(0)
 
@@ -558,6 +566,7 @@
         value = zv[band, :] + beta * dv[band, :]
         dv[band, :] = value
         parts = parts + jnp.sum(value * (tb[0, band, :] + beta * tk[band, :]), axis=0, keepdims=True)
+    leave(dv, do, 2)
     operator_sums(2, qcopy, jnp.zeros((ncrs, LANES), F32), packed(parts), co)
 
     def whole_image(pos, value):
@@ -565,19 +574,9 @@
         wv[band, :] = value + beta * wv[band, :]
 
     operator_end(4, 2, copies, whole_image)
+    leave(wv, wo_out, 3)
     _, energy = late_end(2)
-    alpha = unpacked(rz_next / energy)
-    out_copies = []
-    for pos in range(4):
-        band = slice(pos * FACE, (pos + 1) * FACE)
-        outs[pos] = (mv[band, :] + alpha * dv[band, :])[0:fdof]
-        outs[4 + pos] = (rv[band, :] - alpha * wv[band, :])[0:fdof]
-        for side, ref in enumerate((mo, ro)):
-            copy = pltpu.make_async_copy(outs.at[4 * side + pos], ref.at[0, :, ORDER[pos]], osem.at[4 * side + pos])
-            copy.start()
-            out_copies.append(copy)
-    for copy in out_copies:
-        copy.wait()
+    alpha_out[...] = unpacked(rz_next / energy)
 
     for drain in drains:
         drain()
@@ -616,24 +615,26 @@
         vm((3, LANES, LANES), F32), vm((3, LANES, LANES), F32), vm((LANES, LANES), F32), vm((LANES, LANES), F32),
         vm((2, 24, LANES), F32), vm((3, LANES, cases), F32), vm((3 * LANES, cases), BF16),
         vm((3, 24, LANES), F32), vm((3, 2 * ncrs, 8, LANES), F32), vm((3, chips, 8, LANES), F32),
-        vm((8, cases), F32), vm((8, fdof, cases), F32),
-        dma((8,)), dma((8,)), dma((4, 4)), dma((4, 4)), dma((4,)), dma((4,)), dma((ncrs,)), dma((ncrs,)),
+        vm((8, cases), F32),
+        dma((8,)), dma((16,)), dma((4, 4)), dma((4, 4)), dma((4,)), dma((4,)), dma((ncrs,)), dma((ncrs,)),
     ] + [dma((3,)) for _ in range(14)]
-    out = jax.ShapeDtypeStruct((1, fdof, 4, cases), F32)
+    out = jax.ShapeDtypeStruct((1, SENT, 4, cases), F32)
     anyspace = pl.BlockSpec(memory_space=pl.ANY)
     inside = pl.BlockSpec(memory_space=pltpu.VMEM)
     dims = (nsub, ncrs, nrows, fdof, cases, ncoarse)
-    mult, resid = pl.pallas_call(
+    first, last, resid, image, alpha = pl.pallas_call(
         functools.partial(kernel, dims),
-        out_shape=(out, out),
+        out_shape=(out, out, out, out, jax.ShapeDtypeStruct((1, cases), F32)),
         in_specs=[inside] + [anyspace] * 5,
-        out_specs=(anyspace, anyspace),
+        out_specs=(anyspace, anyspace, anyspace, anyspace, inside),
         scratch_shapes=scratch,
         compiler_params=pltpu.CompilerParams(
             collective_id=0, has_side_effects=True, vmem_limit_bytes=63 * 2**20),
     )(face_index, jnp.swapaxes(kinv, 0, 1), jnp.swapaxes(schur, 0, 1),
       jnp.swapaxes(corner, 1, 2), coarse_inverse, jnp.swapaxes(loads, 0, 1))
-    return jnp.swapaxes(mult, 1, 2), jnp.swapaxes(resid, 1, 2)
+    alpha = alpha[:, None, None, :]
+    first, last, resid, image = (value[:, 0:fdof] for value in (first, last, resid, image))
+    return jnp.swapaxes(first + alpha * last, 1, 2), jnp.swapaxes(resid - alpha * image, 1, 2)
 
 
 def solution(mesh):

time: 86.9 us -> 83.8 us (0.964)
  other arithmetic: 0 us -> 4.41 us
  Pallas kernels: 82.4 us -> 78.6 us
  local copies, waits for them, and re-layouts: 3.63 us -> 0 us
    transpose x0 -> x1, other arithmetic: none -> 4.41 us  [body(): jnp.swapaxes(resid - alpha * image, 1, 2)]
    pallas_call x1, Pallas kernels: 82.4 us -> 78.6 us  [body(): pl.pallas_call(functools.partial(kernel, dims), out_shape=(out, out, out,...]
    unnamed x4 -> x0, local copies, waits for them, and re-layouts: 3.63 us -> none
where the time goes in v6:
time: 83.8 us; the launch traced here: 83.7 us
  Pallas kernels  78.6 us (94%)
  other arithmetic  4.41 us (5%)
    pallas_call x1, Pallas kernels, body(): pl.pallas_call(functools.partial(kernel, dims), out_shape=(out, out, out,...  78.6 us
    transpose x1, other arithmetic, body(): jnp.swapaxes(resid - alpha * image, 1, 2)  4.41 us

profile of v6, /device:TPU:1, one launch (start us, length us, event | category | flops | bytes accessed | tf_op | source)
XLA Modules:
  0.0 83.7 jit_solution(2313745229380187449)
XLA Ops:
  0.6 78.6 %shard_map.77 = (f32[1,152,4,512]{3,2,1,0:T(4,128)}, f32[1,152,4,512]{3,2,1,0:T(4,128)}, f32[1,152,4,512]{3,2,1,0:T(4,128)}, f32[1,152,4,512]{3,2,1,0:T(4,128)}, f32[1,512]{1,0:T(1,128)}) custom-call(s32[1,4,147]{2,1,0:T(4,128)} %faces.1, f32[1215,1,1215]{2,1,0:T(1,128)} %bitcast.9, f32[588,1,588]{2,1,0:T(1,128)} %bitcast.11, f32[1,24,1215]{2,1,0:T(8,128)} %bitcast.12, ...), custom_call_target="tpu_custom_call" | custom-call | tf_op jit(solution)/shard_map/pallas_call | solution.py:625
  79.3 4.4 %subtract_bitcast_fusion = (f32[1,4,147,512]{3,1,2,0:T(4,128)}, f32[1,4,147,512]{3,1,2,0:T(4,128)}) fusion(f32[1,152,4,512]{3,2,1,0:T(4,128)} %get-tuple-element.11, f32[1,152,4,512]{3,2,1,0:T(4,128)} %get-tuple-element.10, f32[512]{0:T(512)} %bitcast.13, f32[1,152,4,512]{3,2,1,0:T(4,128)} %get-tuple-element.9, f32[1,152,4,512]{3,2,1,0:T(4,128)} %get-tuple-element.7), kind=kLoop, calls=%fused_computation | loop fusion | flops 1204224 | bytes 7227392 | tf_op jit(solution)/shard_map/transpose | solution.py:637

commit v7 on v6

--- a/solution.py
+++ b/solution.py
@@ -64,13 +64,13 @@
     cbp, ncp = cip.shape
     a = lax.axis_index("sub")
     b = lax.axis_index("crs")
-    k = lax.div(a, 2)
-    c = lax.rem(a, 2)
+    k = a >> 1
+    c = a & 1
     sib = 2 * k + 1 - c
-    up = lax.rem(a + 1, nsub)
-    down = lax.rem(a + nsub - 1, nsub)
-    left = lax.rem(b + ncrs - 1, ncrs)
-    right = lax.rem(b + 1, ncrs)
+    up = (a + 1) & (nsub - 1)
+    down = (a + nsub - 1) & (nsub - 1)
+    left = (b + ncrs - 1) & (ncrs - 1)
+    right = (b + 1) & (ncrs - 1)
     dests = ((a, left), (a, right), (down, b), (up, b))
     keeps = (None, None, a > 0, a < nsub - 1)
     drains = []
@@ -93,17 +93,17 @@
 
     barrier = pltpu.get_barrier_semaphore()
     for j in range(1, ncrs):
-        pl.semaphore_signal(barrier, inc=1, device_id=(a, lax.rem(b + j, ncrs)), device_id_type=MESH)
+        pl.semaphore_signal(barrier, inc=1, device_id=(a, (b + j) & (ncrs - 1)), device_id_type=MESH)
     for j in range(ncrs):
         pl.semaphore_signal(barrier, inc=1, device_id=(up, j), device_id_type=MESH)
         pl.semaphore_signal(barrier, inc=1, device_id=(down, j), device_id_type=MESH)
     for j in range(1, ncrs):
-        to = lax.rem(b + j, ncrs)
-        pl.semaphore_signal(barrier, inc=1, device_id=(lax.rem(a + 2, nsub), to), device_id_type=MESH)
-        pl.semaphore_signal(barrier, inc=1, device_id=(lax.rem(a + nsub - 2, nsub), to), device_id_type=MESH)
+        to = (b + j) & (ncrs - 1)
+        pl.semaphore_signal(barrier, inc=1, device_id=((a + 2) & (nsub - 1), to), device_id_type=MESH)
+        pl.semaphore_signal(barrier, inc=1, device_id=((a + nsub - 2) & (nsub - 1), to), device_id_type=MESH)
 
     def greet(j, carry):
-        pl.semaphore_signal(barrier, inc=1, device_id=(2 * lax.rem(k + j, chips) + c, b), device_id_type=MESH)
+        pl.semaphore_signal(barrier, inc=1, device_id=(2 * ((k + j) & (chips - 1)) + c, b), device_id_type=MESH)
         return carry
 
     lax.fori_loop(1, chips, greet, 0)
@@ -153,7 +153,7 @@
     da = div(l, 12)
     rem12 = l - 12 * da
     db = div(rem12, 6)
-    where_l = jnp.where(l < 24, 24 * da + 6 * lax.rem(b + db, ncrs) + rem12 - 6 * db, -1000)
+    where_l = jnp.where(l < 24, 24 * da + 6 * ((b + db) & (ncrs - 1)) + rem12 - 6 * db, -1000)
     sel = hot(where_l == rows_of((NC, 32)))
     a0hi[0:NC, :] = dot(sel, chi).astype(BF16)
     a0lo[0:NC, :] = dot(sel, clo).astype(BF16)
@@ -180,9 +180,9 @@
 
     def coarse_begin(f, offs):
         for i, off in enumerate(offs):
-            owner = lax.rem(a + off + nsub, nsub)
+            owner = (a + off + nsub) & (nsub - 1)
             for j in range(ncrs):
-                to = lax.rem(b + j, ncrs)
+                to = (b + j) & (ncrs - 1)
                 at = pl.ds(pl.multiple_of(to * LANES, LANES), LANES)
                 band = pl.ds(24 * i, 24)
                 if off == 0 and j == 0:
@@ -197,7 +197,7 @@
         gb[f, k] = jnp.sum(p0[f, 0:count], axis=0)
 
         def send(j, carry):
-            to = 2 * lax.rem(k + j, chips) + c
+            to = 2 * ((k + j) & (chips - 1)) + c
             remote(gb.at[f, k], gb.at[f, k], s2s.at[f], s2r.at[f], (to, b)).start()
             return carry
 
@@ -223,7 +223,7 @@
         hb[f, 0:NW, at] = hs[pl.ds(pl.multiple_of(24 * c, 8), NW), :]
         for j in range(1, ncrs):
             remote(hb.at[f, pl.ds(0, NW), at], hb.at[f, pl.ds(0, NW), at], s3s.at[f], s3r.at[f],
-                   (a, lax.rem(b + j, ncrs))).start()
+                   (a, (b + j) & (ncrs - 1))).start()
         drains.append(lambda: settle(hb.at[f, pl.ds(0, NW), pl.ds(0, (ncrs - 1) * LANES)], s3s.at[f]))
 
     def coarse_energy(f, qcopy, scale=None):
@@ -261,7 +261,7 @@
         er[n, k] = jnp.concatenate([first, second], axis=0)
 
         def send(j, carry):
-            to = 2 * lax.rem(k + j, chips) + c
+            to = 2 * ((k + j) & (chips - 1)) + c
             remote(er.at[n, k], er.at[n, k], r2s.at[n], r2r.at[n], (to, b)).start()
             return carry
 
@@ -276,7 +276,7 @@
             for j in range(ncrs):
                 if cc == 0 and j == 0:
                     continue
-                dev = (a if cc == 0 else sib, lax.rem(b + j, ncrs))
+                dev = (a if cc == 0 else sib, (b + j) & (ncrs - 1))
                 remote(mine, mine, r1s.at[n], r1r.at[n], dev).start()
         drains.append(lambda: settle(rr.at[n, pl.ds(0, 2 * ncrs - 1)], r1s.at[n]))
 
@@ -338,7 +338,7 @@
     sel = hot(r == cols_of((LANES, ncp)))
     dall[b] = dot_nt(sel, x1h) + dot_nt(sel, x1l)
     for j in range(1, ncrs):
-        remote(dall.at[b], dall.at[b], csend.at[j], crecv.at[j], (a, lax.rem(b + j, ncrs))).start()
+        remote(dall.at[b], dall.at[b], csend.at[j], crecv.at[j], (a, (b + j) & (ncrs - 1))).start()
 
     bch = dot_nt(bmat[...], chi).astype(BF16)
     bcl = dot_nt(bmat[...], clo).astype(BF16)
@@ -346,7 +346,7 @@
     da = div(l, 12)
     rem12 = l - 12 * da
     db = div(rem12, 6)
-    where_l = 24 * (1 + da) + 6 * lax.rem(b + db, ncrs) + rem12 - 6 * db
+    where_l = 24 * (1 + da) + 6 * ((b + db) & (ncrs - 1)) + rem12 - 6 * db
     where_l = jnp.where(l < 24, where_l, -1000)
     lanes = cols_of((32, LANES))
     emaps = [hot(where_l + off == lanes) for off in (0, 24, -24)]
@@ -362,18 +362,7 @@
 
     in_copies[3].wait()
 
-    def split_k(i, carry):
-        at = pl.multiple_of(i * step, step)
-        high, low = split(kv[pl.ds(at, step), :])
-        khi[pl.ds(at, step), 0:nrows] = high
-        klo[pl.ds(at, step), 0:nrows] = low
-        return carry
-
-    lax.fori_loop(0, whole // step, split_k, 0)
     tail[0:left_rows, 0:nrows] = kv[whole:nrows, :]
-    high, low = split(tail[...])
-    khi[whole:whole + 16, :] = high
-    klo[whole:whole + 16, :] = low
 
     def face_rows(lo, hi):
         def tile(i, carry):
@@ -385,7 +374,17 @@
         lax.fori_loop(0, nrp // 256, tile, 0)
 
     half = 2 * FACE
-    face_rows(0, half)
+    for i in range(nrp // 256):
+        at = slice(i * 256, (i + 1) * 256)
+        filled = slice(i * 256, min((i + 1) * 256, nrows))
+        high, low = split(kv[0:whole, filled])
+        khi[0:whole, filled] = high
+        klo[0:whole, filled] = low
+        high, low = split(tail[:, at])
+        khi[whole:whole + 16, at] = high
+        klo[whole:whole + 16, at] = low
+        a0hi[NC:NC + half, at] = dot(bmat[0:half, :], khi[:, at]).astype(BF16)
+        a0lo[NC:NC + half, at] = dot(bmat[0:half, :], klo[:, at]).astype(BF16)
     tb[0, 0:half, :] = apply_loads(NC, NC + half)
     copies = faces_start(0, (0, 1))
     qcopy = coarse_gather(0, (0, 1))
@@ -394,7 +393,7 @@
     copies += faces_start(0, (2, 3))
 
     for j in range(1, ncrs):
-        copy = remote(dall.at[b], dall.at[b], csend.at[j], crecv.at[j], (a, lax.rem(b + j, ncrs)))
+        copy = remote(dall.at[b], dall.at[b], csend.at[j], crecv.at[j], (a, (b + j) & (ncrs - 1)))
         copy.wait()
     total_hi = total_lo = None
     for blk_b in range(ncrs):
@@ -486,15 +485,17 @@
     around = (-1, 0, 1, 2)
 
     halves = (slice(0, cases // 2), slice(cases // 2, cases))
-    every = (0, 1, 2, 3)
 
     def precond(n, f):
         block = dot(m3[0:NW + half, :], x3[...])
         pbuf[f] = block[0:NW]
         coarse_begin(f, around)
         tb[n % 2, 0:half, :] = block[NW:]
+        copies = [faces_start(n, (0, 1), lanes, h) for h, lanes in enumerate(halves)]
         tb[n % 2, half:, :] = dot(m3[NW + half:, :], x3[...])
-        return [faces_start(n, every, lanes, h) for h, lanes in enumerate(halves)]
+        for h, lanes in enumerate(halves):
+            copies[h] += faces_start(n, (2, 3), lanes, h)
+        return copies
 
     def operator(n, copies, keep_z):
         out = []
@@ -505,8 +506,9 @@
                 keep_z[pos * FACE:(pos + 1) * FACE, lanes] = value
                 put_x(pos, value, lanes)
             tb[n % 2, 0:half, lanes] = dot(a3[0:half, :], x3[:, lanes])
+            out += faces_start(n, (0, 1), lanes, h)
             tb[n % 2, half:, lanes] = dot(a3[half:, :], x3[:, lanes])
-            out += faces_start(n, every, lanes, h)
+            out += faces_start(n, (2, 3), lanes, h)
         return out
 
     def operator_sums(f, qcopy, rz_part, energy, scale):

time: 83.8 us -> 81.6 us (0.974)
  Pallas kernels: 78.6 us -> 76.4 us
    pallas_call x1, Pallas kernels: 78.6 us -> 76.4 us  [body(): pl.pallas_call(functools.partial(kernel, dims), out_shape=(out, out, out,...]
where the time goes in v7:
time: 81.6 us; the launch traced here: 81.4 us
  Pallas kernels  76.4 us (94%)
  other arithmetic  4.41 us (5%)
    pallas_call x1, Pallas kernels, body(): pl.pallas_call(functools.partial(kernel, dims), out_shape=(out, out, out,...  76.4 us
    transpose x1, other arithmetic, body(): jnp.swapaxes(resid - alpha * image, 1, 2)  4.41 us

profile of v7, /device:TPU:1, one launch (start us, length us, event | category | flops | bytes accessed | tf_op | source)
XLA Modules:
  0.0 81.4 jit_solution(4364809482737814955)
XLA Ops:
  0.6 76.4 %shard_map.77 = (f32[1,152,4,512]{3,2,1,0:T(4,128)}, f32[1,152,4,512]{3,2,1,0:T(4,128)}, f32[1,152,4,512]{3,2,1,0:T(4,128)}, f32[1,152,4,512]{3,2,1,0:T(4,128)}, f32[1,512]{1,0:T(1,128)}) custom-call(s32[1,4,147]{2,1,0:T(4,128)} %faces.1, f32[1215,1,1215]{2,1,0:T(1,128)} %bitcast.9, f32[588,1,588]{2,1,0:T(1,128)} %bitcast.11, f32[1,24,1215]{2,1,0:T(8,128)} %bitcast.12, ...), custom_call_target="tpu_custom_call" | custom-call | tf_op jit(solution)/shard_map/pallas_call | solution.py:627
  77.0 4.4 %subtract_bitcast_fusion = (f32[1,4,147,512]{3,1,2,0:T(4,128)}, f32[1,4,147,512]{3,1,2,0:T(4,128)}) fusion(f32[1,152,4,512]{3,2,1,0:T(4,128)} %get-tuple-element.11, f32[1,152,4,512]{3,2,1,0:T(4,128)} %get-tuple-element.10, f32[512]{0:T(512)} %bitcast.13, f32[1,152,4,512]{3,2,1,0:T(4,128)} %get-tuple-element.9, f32[1,152,4,512]{3,2,1,0:T(4,128)} %get-tuple-element.7), kind=kLoop, calls=%fused_computation | loop fusion | flops 1204224 | bytes 7227392 | tf_op jit(solution)/shard_map/transpose | solution.py:639

commit v8 on v7

--- a/solution.py
+++ b/solution.py
@@ -53,7 +53,7 @@
 def kernel(dims, faces, kinv, schur, corner, cinv, loads, mo, do, ro, wo_out, alpha_out,
            kv, lv, cv, sv, civ, khi, klo, tail, idxr, idxc, bmat, bmt, a0hi, a0lo, lhi, llo, a3, m3, w3, x3,
            cpad, cip, sp, tmt, ws, wo, wr, dall, dphi, dplo,
-           tb, rb, rv, dv, mv, zv, tk, wv, pbuf, p0, gb, sibs, sibr, hs, hk, qk, hb, h3,
+           tb, rb, rv, dv, mv, zv, tk, wv, pw, pbuf, p0, gb, sibs, sibr, hs, hk, qk, hb, h3,
            qs, rr, er, co,
            dsem, osem, fsend, frecv, wsend, wrecv, csend, crecv,
            s1s, s1r, s2s, s2r, bs, br, s3s, s3r, r1s, r1r, r2s, r2r, qsend, qrecv):
@@ -540,15 +540,26 @@
         wv[pos * FACE:(pos + 1) * FACE, :] = value
 
     operator_end(2, 1, copies, keep_image)
+    largest = jnp.max(jnp.abs(wv[...]), axis=0, keepdims=True)
+    largest = jnp.where(largest > 0.0, largest, 1.0)
+    for pos in range(4):
+        put_x(pos, wv[pos * FACE:(pos + 1) * FACE, :] / largest)
+    block = dot(m3[0:NW + half, :], x3[...])
+    pw[...] = block[0:NW]
+    zv[0:half, :] = block[NW:]
+    zv[half:, :] = dot(m3[NW + half:, :], x3[...])
     rz_now, energy = late_end(1)
     alpha = unpacked(rz_now / energy)
-    for pos in range(4):
-        band = slice(pos * FACE, (pos + 1) * FACE)
-        value = rv[band, :] - alpha * wv[band, :]
-        rv[band, :] = value
-        put_x(pos, value)
-
-    copies = precond(3, 2)
+
+    moved = alpha * largest
+    pbuf[2] = pbuf[1] - moved * pw[...]
+    coarse_begin(2, around)
+    tb[1, 0:half, :] = tb[1, 0:half, :] - moved * zv[0:half, :]
+    copies = [faces_start(3, (0, 1), lanes, h) for h, lanes in enumerate(halves)]
+    tb[1, half:, :] = tb[1, half:, :] - moved * zv[half:, :]
+    for h, lanes in enumerate(halves):
+        copies[h] += faces_start(3, (2, 3), lanes, h)
+    rv[...] = rv[...] - alpha * wv[...]
     late_begin(0, total_rz(3), jnp.zeros((ncrs, LANES), F32))
     for pos in range(4):
         band = slice(pos * FACE, (pos + 1) * FACE)
@@ -613,7 +624,7 @@
         vm((2, NX, cases), F32), vm((2, 4, FACE, cases), F32),
         vm((NX, cases), F32), vm((NX, cases), F32), vm((NX, cases), F32),
         vm((NX, cases), F32), vm((NX, cases), F32), vm((NX, cases), F32),
-        vm((3, NW, cases), F32), vm((3, 4 * ncrs, 24, LANES), F32), vm((3, chips, 24, LANES), F32),
+        vm((NW, cases), F32), vm((3, NW, cases), F32), vm((3, 4 * ncrs, 24, LANES), F32), vm((3, chips, 24, LANES), F32),
         vm((3, LANES, LANES), F32), vm((3, LANES, LANES), F32), vm((LANES, LANES), F32), vm((LANES, LANES), F32),
         vm((2, 24, LANES), F32), vm((3, LANES, cases), F32), vm((3 * LANES, cases), BF16),
         vm((3, 24, LANES), F32), vm((3, 2 * ncrs, 8, LANES), F32), vm((3, chips, 8, LANES), F32),

time: 81.6 us -> 80.5 us (0.987)
  Pallas kernels: 76.4 us -> 75.3 us
    pallas_call x1, Pallas kernels: 76.4 us -> 75.3 us  [body(): pl.pallas_call(functools.partial(kernel, dims), out_shape=(out, out, out,...]
where the time goes in v8:
time: 80.5 us; the launch traced here: 80.4 us
  Pallas kernels  75.3 us (94%)
  other arithmetic  4.41 us (5%)
    pallas_call x1, Pallas kernels, body(): pl.pallas_call(functools.partial(kernel, dims), out_shape=(out, out, out,...  75.3 us
    transpose x1, other arithmetic, body(): jnp.swapaxes(resid - alpha * image, 1, 2)  4.41 us

profile of v8, /device:TPU:1, one launch (start us, length us, event | category | flops | bytes accessed | tf_op | source)
XLA Modules:
  0.0 80.4 jit_solution(3500279550036189121)
XLA Ops:
  0.6 75.3 %shard_map.77 = (f32[1,152,4,512]{3,2,1,0:T(4,128)}, f32[1,152,4,512]{3,2,1,0:T(4,128)}, f32[1,152,4,512]{3,2,1,0:T(4,128)}, f32[1,152,4,512]{3,2,1,0:T(4,128)}, f32[1,512]{1,0:T(1,128)}) custom-call(s32[1,4,147]{2,1,0:T(4,128)} %faces.1, f32[1215,1,1215]{2,1,0:T(1,128)} %bitcast.9, f32[588,1,588]{2,1,0:T(1,128)} %bitcast.11, f32[1,24,1215]{2,1,0:T(8,128)} %bitcast.12, ...), custom_call_target="tpu_custom_call" | custom-call | tf_op jit(solution)/shard_map/pallas_call | solution.py:638
  75.9 4.4 %subtract_bitcast_fusion = (f32[1,4,147,512]{3,1,2,0:T(4,128)}, f32[1,4,147,512]{3,1,2,0:T(4,128)}) fusion(f32[1,152,4,512]{3,2,1,0:T(4,128)} %get-tuple-element.11, f32[1,152,4,512]{3,2,1,0:T(4,128)} %get-tuple-element.10, f32[512]{0:T(512)} %bitcast.13, f32[1,152,4,512]{3,2,1,0:T(4,128)} %get-tuple-element.9, f32[1,152,4,512]{3,2,1,0:T(4,128)} %get-tuple-element.7), kind=kLoop, calls=%fused_computation | loop fusion | flops 1204224 | bytes 7227392 | tf_op jit(solution)/shard_map/transpose | solution.py:650
